TPU v7x, 32 devices: a whole 2x2x4 slice. The times are simulated.
32 devices in a mesh: dp: 4 (over z), tm: 4 (over y, core), head: 2 (over x).
Axes of the slice: x: 2, y: 2, z: 4, core: 2. Of those that a mesh axis runs over, the one named last changes fastest.
Arguments:
- queries: bfloat16 [128, 32, 3072], P(('dp', 'tm'), None, 'head'), parts along dimension 0, may hold values from -16 to 16
- keys: bfloat16 [128, 32, 3072], P(('dp', 'tm'), None, 'head'), parts along dimension 0, may hold values from -16 to 16
- values: bfloat16 [128, 32, 3072], P(('dp', 'tm'), None, 'head'), parts along dimension 0, may hold values from -6 to 6
- out_grad: bfloat16 [128, 32, 3072], P(('dp', 'tm'), None, 'head'), parts along dimension 0, may hold values from -6 to 6
- out_weight: bfloat16 [3072, 3072], P('tm', 'head'), may hold values from -0.109375 to 0.109375
- lists: int32 [32, 8], P(('dp', 'tm')), parts along dimension 0, may hold values from 0 to 31, as said below
Outputs:
- query_grad: bfloat16 [128, 32, 3072], P(('dp', 'tm'), None, 'head'), parts along dimension 0
- key_grad: bfloat16 [128, 32, 3072], P(('dp', 'tm'), None, 'head'), parts along dimension 0
- value_grad: bfloat16 [128, 32, 3072], P(('dp', 'tm'), None, 'head'), parts along dimension 0
- weight_grad: float32 [12288, 3072], P(('dp', 'tm'), 'head'), parts along dimension 0
There are 4 independent parts, one for each index of `dp`. A program takes and returns all parts, laid end to end along the dimension named above; an argument that names none is the same for every part. Nothing has to cross between parts.
Inputs may be any that keep to these rules, and one draw needn't show every extreme that they name: `lists`: each group names 8 different frames of its rollout. Among the 4 list entries of one time shard's groups, at most 4 name frames owned by any one time shard, and those name at most 2 distinct frame; in every draw, every time shard has some owner for which both bounds are reached.
All inputs are finite; a program needn't handle non-finite values.
Results may differ from a plain program's by a relative error of at most 0.039.
Values may be sent and summed in bfloat16 or wider, within the bound.
A program may use at most 128 MiB of HBM per device.

v0:
```python
import jax
import jax.numpy as jnp
from jax import lax
from jax.sharding import PartitionSpec as P

HD = 128
CF = 4
RET = 8


def slot_tables(owners, local_frame, slot_index, occupied, myself, capacity):
    slot_range = jnp.arange(capacity, dtype=jnp.int32)
    matches = (
        occupied[:, None, :]
        & (owners[:, None, :] == myself)
        & (slot_index[:, None, :] == slot_range[None, :, None])
    )
    source = jnp.sum(jnp.where(matches, local_frame[:, None, :], 0), axis=2)
    filled = jnp.any(matches, axis=2)
    return (source.reshape(-1), filled.reshape(-1))


def pack_slots(frame_rows, source, filled):
    picked = jnp.take(frame_rows, source, axis=0)
    return jnp.where(filled[:, None, None], picked, jnp.zeros_like(picked))


def per_device(queries, keys, values, out_grad, out_weight, lists):
    frames_dev, frame_tokens, width = queries.shape
    heads_dev = width // HD
    tm_count = lax.axis_size("tm")
    myself = lax.axis_index("tm")
    groups_dev = frames_dev // CF
    entry_count = groups_dev * RET
    token_rows = frames_dev * frame_tokens
    group_rows = CF * frame_tokens
    score_factor = HD ** (-0.5)
    per_owner = max(1, RET // tm_count)
    every_list = lax.all_gather(lists, "tm", axis=0, tiled=True)
    wanted = every_list.reshape(tm_count, entry_count)
    owners = wanted // frames_dev
    local_frame = wanted - owners * frames_dev
    position = jnp.arange(entry_count, dtype=jnp.int32)
    before = (position[:, None] < position[None, :])[None]
    same_owner = owners[:, :, None] == owners[:, None, :]
    same_frame = wanted[:, :, None] == wanted[:, None, :]
    first_seen = jnp.logical_not(jnp.any(same_frame & before, axis=1))
    entry_slot = jnp.sum(same_owner & before, axis=1)
    frame_first = jnp.sum(same_owner & before & first_seen[:, :, None], axis=1)
    frame_slot = jnp.sum(
        jnp.where(same_frame & first_seen[:, :, None], frame_first[:, :, None], 0), axis=1
    )
    my_owner = lax.dynamic_index_in_dim(owners, myself, 0, keepdims=False)
    my_entry_slot = lax.dynamic_index_in_dim(entry_slot, myself, 0, keepdims=False)
    my_frame_slot = lax.dynamic_index_in_dim(frame_slot, myself, 0, keepdims=False)
    frame_source, frame_filled = slot_tables(
        owners, local_frame, frame_slot, first_seen, myself, per_owner
    )
    capacity = groups_dev * per_owner
    source, filled = slot_tables(
        owners, local_frame, entry_slot, jnp.ones_like(first_seen), myself, capacity
    )
    got_keys, got_values = (
        lax.all_to_all(
            pack_slots(keys, source, filled), "tm", split_axis=0, concat_axis=0, tiled=True
        ),
        lax.all_to_all(
            pack_slots(values, source, filled), "tm", split_axis=0, concat_axis=0, tiled=True
        ),
    )
    lookup = my_owner * capacity + my_entry_slot
    grad_full = lax.all_gather(out_grad, "head", axis=2, tiled=True)
    grad_rows = grad_full.reshape(token_rows, grad_full.shape[2])
    columns = grad_rows
    attn_grad = jnp.dot(
        columns,
        lax.all_gather(out_weight, "tm", axis=0, tiled=True),
        preferred_element_type=jnp.float32,
    ).astype(jnp.bfloat16)
    far_keys = jnp.take(got_keys, lookup, axis=0)
    far_values = jnp.take(got_values, lookup, axis=0)
    far_span = RET * frame_tokens
    query_blocks = queries.reshape(groups_dev, group_rows, heads_dev, HD)
    key_set = jnp.concatenate(
        [
            keys.reshape(groups_dev, group_rows, heads_dev, HD),
            far_keys.reshape(groups_dev, far_span, heads_dev, HD),
        ],
        axis=1,
    )
    value_set = jnp.concatenate(
        [
            values.reshape(groups_dev, group_rows, heads_dev, HD),
            far_values.reshape(groups_dev, far_span, heads_dev, HD),
        ],
        axis=1,
    )
    scores = (
        jnp.einsum("cqhd,ckhd->chqk", query_blocks, key_set, preferred_element_type=jnp.float32)
        * score_factor
    )
    row_top = jnp.max(scores, axis=3, keepdims=True)
    weighted = jnp.exp(scores - row_top)
    prob = weighted / jnp.sum(weighted, axis=3, keepdims=True)
    prob_low = prob.astype(jnp.bfloat16)
    attn_out = jnp.einsum(
        "chqk,ckhd->cqhd", prob_low, value_set, preferred_element_type=jnp.float32
    ).astype(jnp.bfloat16)
    grad_blocks = attn_grad.reshape(groups_dev, group_rows, heads_dev, HD)
    row_dot = jnp.sum(grad_blocks.astype(jnp.float32) * attn_out.astype(jnp.float32), axis=3)
    row_dot = jnp.transpose(row_dot, (0, 2, 1))[..., None]
    prob_grad = jnp.einsum(
        "cqhd,ckhd->chqk", grad_blocks, value_set, preferred_element_type=jnp.float32
    )
    score_grad = (prob * (prob_grad - row_dot)).astype(jnp.bfloat16)
    query_grad = (
        jnp.einsum("chqk,ckhd->cqhd", score_grad, key_set, preferred_element_type=jnp.float32)
        * score_factor
    ).astype(jnp.bfloat16)
    key_term = (
        jnp.einsum("chqk,cqhd->ckhd", score_grad, query_blocks, preferred_element_type=jnp.float32)
        * score_factor
    )
    value_term = jnp.einsum(
        "chqk,cqhd->ckhd", prob_low, grad_blocks, preferred_element_type=jnp.float32
    )
    own_dk = key_term[:, :group_rows].reshape(frames_dev, frame_tokens, width)
    own_dv = value_term[:, :group_rows].reshape(frames_dev, frame_tokens, width)
    far_dk = key_term[:, group_rows:].reshape(entry_count, frame_tokens, width)
    far_dv = value_term[:, group_rows:].reshape(entry_count, frame_tokens, width)
    back_slot = my_owner * per_owner + my_frame_slot
    empty = jnp.zeros((tm_count * per_owner, frame_tokens, width), jnp.float32)
    back_keys = empty.at[back_slot].add(far_dk).astype(jnp.bfloat16)
    back_values = empty.at[back_slot].add(far_dv).astype(jnp.bfloat16)
    came_keys, came_values = (
        lax.all_to_all(back_keys, "tm", split_axis=0, concat_axis=0, tiled=True),
        lax.all_to_all(back_values, "tm", split_axis=0, concat_axis=0, tiled=True),
    )
    selector = (
        (frame_source[None, :] == jnp.arange(frames_dev, dtype=jnp.int32)[:, None])
        & frame_filled[None, :]
    ).astype(jnp.bfloat16)
    into_keys = jnp.dot(
        selector, came_keys.reshape(tm_count * per_owner, -1), preferred_element_type=jnp.float32
    )
    into_values = jnp.dot(
        selector, came_values.reshape(tm_count * per_owner, -1), preferred_element_type=jnp.float32
    )
    key_grad = (own_dk + into_keys.reshape(frames_dev, frame_tokens, width)).astype(jnp.bfloat16)
    value_grad = (own_dv + into_values.reshape(frames_dev, frame_tokens, width)).astype(
        jnp.bfloat16
    )
    attn_rows = attn_out.reshape(token_rows, width)
    columns = grad_rows
    weight_grad = lax.psum_scatter(
        lax.dot_general(
            columns, attn_rows, (((0,), (0,)), ((), ())), preferred_element_type=jnp.float32
        ).astype(jnp.bfloat16),
        "tm",
        scatter_dimension=0,
        tiled=True,
    ).astype(jnp.float32)
    return (query_grad.reshape(frames_dev, frame_tokens, width), key_grad, value_grad, weight_grad)


def solution(mesh):
    return jax.shard_map(
        per_device,
        mesh=mesh,
        in_specs=(
            P(("dp", "tm"), None, "head"),
            P(("dp", "tm"), None, "head"),
            P(("dp", "tm"), None, "head"),
            P(("dp", "tm"), None, "head"),
            P("tm", "head"),
            P(("dp", "tm"), None),
        ),
        out_specs=(
            P(("dp", "tm"), None, "head"),
            P(("dp", "tm"), None, "head"),
            P(("dp", "tm"), None, "head"),
            P(("dp", "tm"), "head"),
        ),
        check_vma=False,
    )
```

profile of v0, /device:TPU:1, one launch (start us, length us, event | category | flops | bytes accessed | tf_op | source)
XLA Modules:
  0.0 249.5 jit_solution(13808224770981572753)
XLA Ops:
  8.7 5.9 %all-gather = s32[4,2,8]{2,1,0:T(2,128)S(1)} all-gather(s32[1,2,8]{2,1,0:T(2,128)S(1)} %bitcast.98), channel_id=1, replica_groups=mesh['dp'=4,'tm'=4,'head'=2] {'tm'}, dimensions={0}, use_global_device_ids=true | all-gather | bytes 320 | tf_op jit(solution)/shard_map/all_gather | solution.py:39
  21.0 23.0 %all_to_all.20 = bf16[16,32,1536]{2,1,0:T(8,128)(2,1)} all-to-all(bf16[16,32,1536]{2,1,0:T(8,128)(2,1)S(1)} %get-tuple-element.29), channel_id=1, replica_groups=mesh['dp'=4,'tm'=4,'head'=2] {'tm'}, dimensions={0} | all-to-all | bytes 3145728 | tf_op jit(solution)/shard_map/all_to_all | solution.py:67
  44.0 5.0 %all-to-all-start = ((bf16[16,32,1536]{2,1,0:T(8,128)(2,1)}), bf16[16,32,1536]{2,1,0:T(8,128)(2,1)}, u32[]{:S(2)}, u32[]{:S(2)}) async-start(bf16[16,32,1536]{2,1,0:T(8,128)(2,1)} %get-tuple-element.30), calls=%async_computation | async-start | bytes 3145728 | tf_op jit(solution)/shard_map/all_to_all | solution.py:64
  58.7 25.2 %all-to-all-done = bf16[16,32,1536]{2,1,0:T(8,128)(2,1)} async-done(((bf16[16,32,1536]{2,1,0:T(8,128)(2,1)}), bf16[16,32,1536]{2,1,0:T(8,128)(2,1)}, u32[]{:S(2)}, u32[]{:S(2)}) %all-to-all-start) | async-done | bytes 1572896 | tf_op jit(solution)/shard_map/all_to_all | solution.py:64
  87.1 4.0 %broadcast_select_fusion = (bf16[16,32,1536]{2,1,0:T(8,128)(2,1)}, bf16[16,32,1536]{2,1,0:T(8,128)(2,1)}) fusion(bf16[16,32,1536]{2,1,0:T(8,128)(2,1)} %gather_fusion.3, pred[16]{0:T(512)(128)(4,1)S(1)} %get-tuple-element.27, bf16[16,32,1536]{2,1,0:T(8,128)(2,1)} %gather_fusion.1), kind=kLoop, calls=%fused_computation.31 | loop fusion | flops 1572864 | bytes 6291472 | tf_op jit(solution)/shard_map/jit(_take)/select_n | solution.py:81
  91.1 4.0 %reshape.232 = bf16[2,256,12,128]{3,2,1,0:T(8,128)(2,1)} reshape(bf16[16,32,1536]{2,1,0:T(8,128)(2,1)} %get-tuple-element.32) | data formatting | bytes 3145728 | tf_op jit(solution)/shard_map/reshape | solution.py:87
  95.0 3.9 %reshape.237 = bf16[2,256,12,128]{3,2,1,0:T(8,128)(2,1)} reshape(bf16[16,32,1536]{2,1,0:T(8,128)(2,1)} %get-tuple-element.31) | data formatting | bytes 3145728 | tf_op jit(solution)/shard_map/reshape | solution.py:94
  106.3 3.4 %fusion.49 = (f32[2,12,128]{2,1,0:T(8,128)S(1)}, f32[2,12,128,384]{2,3,1,0:T(8,128)}) fusion(f32[2,12,384,128]{3,2,1,0:T(8,128)S(1)} %fusion.16), kind=kOutput, calls=%fused_computation.92 | output fusion | flops 4718975 | bytes 9449472 | tf_op jit(solution)/shard_map/sub | solution.py:103
  109.7 11.5 %all-gather.6.cloned.1.call-done = bf16[3072,1536]{1,0:T(8,128)(2,1)} async-done(((bf16[768,1536]{1,0:T(8,128)(2,1)}), bf16[3072,1536]{1,0:T(8,128)(2,1)}) %all-gather.6.cloned.1.call-update) | async-done | bytes 9437200 | tf_op jit(solution)/shard_map/all_gather | solution.py:77
  121.2 6.8 %convolution_convert_fusion.1 = bf16[256,1536]{1,0:T(8,128)(2,1)S(1)} fusion(bf16[256,3072]{1,0:T(8,128)(2,1)} %bitcast.96, bf16[3072,1536]{1,0:T(8,128)(2,1)} %all-gather.6.cloned.1.call-done), kind=kOutput, calls=%fused_computation.18 | convolution fusion | flops 2416312320 | bytes 11796480 | tf_op jit(solution)/shard_map/dot_general | solution.py:75
  129.3 7.0 %multiply_reduce_fusion = (f32[2,128,12]{1,2,0:T(8,128)S(1)}, bf16[2,128,12,128]{1,3,2,0:T(8,128)(2,1)S(1)}) fusion(bf16[2,128,12,128]{1,3,2,0:T(8,128)(2,1)S(1)} %copy.85, bf16[2,384,12,128]{3,1,2,0:T(8,128)(2,1)} %copy_dynamic-update-slice_fusion, f32[2,12,128]{2,1,0:T(8,128)S(1)} %get-tuple-element.34, f32[2,12,384,128]{3,2,1,0:T(8,128)} %copy-done), kind=kOutput, calls=%fused_computation.30 | convolution fusion | flops 309854592 | bytes 8675328 | tf_op jit(solution)/shard_map/chqk,ckhd->cqhd/dot_general | solution.py:106
  137.8 5.0 %fusion.1 = bf16[3072,1536]{0,1:T(8,128)(2,1)} fusion(bf16[256,3072]{1,0:T(8,128)(2,1)S(1)} %bitcast.97, bf16[192,8,2,128]{3,2,1,0:T(2,128)(2,1)S(1)} %bitcast.95), kind=kOutput, calls=%fused_computation.8 | convolution fusion | flops 2420637696 | bytes 11796480 | tf_op jit(solution)/shard_map/dot_general | solution.py:156
  142.9 3.9 %multiply_convert_fusion = bf16[2,12,128,384]{2,3,1,0:T(8,128)(2,1)S(1)} fusion(f32[2,12,128]{2,1,0:T(8,128)S(1)} %bitcast.99, bf16[2,384,12,128]{3,1,2,0:T(8,128)(2,1)} %copy_dynamic-update-slice_fusion, bf16[2,128,12,128]{1,3,2,0:T(8,128)(2,1)S(1)} %copy.85, f32[2,12,128,384]{2,3,1,0:T(8,128)} %get-tuple-element.35, f32[2,12,128]{2,1,0:T(8,128)S(1)} %get-tuple-element.34), kind=kOutput, calls=%fused_computation.14 | convolution fusion | flops 306708480 | bytes 10248192 | tf_op jit(solution)/shard_map/cqhd,ckhd->chqk/dot_general | solution.py:112
  151.5 4.4 %copy.96 = f32[2,256,12,128]{3,2,1,0:T(8,128)} copy(f32[2,256,12,128]{3,1,2,0:T(8,128)S(1)} %slice.25) | data formatting | bytes 6291456 | tf_op jit(solution)/shard_map/slice | solution.py:129
  155.8 5.1 %reshape.282 = f32[16,32,1536]{2,1,0:T(8,128)} reshape(f32[2,256,12,128]{3,2,1,0:T(8,128)} %copy.96) | data formatting | bytes 6291456 | tf_op jit(solution)/shard_map/reshape | solution.py:129
  161.2 5.3 %scatter_fusion = f32[8,32,1536]{2,1,0:T(8,128)S(1)} fusion(f32[8,32,1536]{2,1,0:T(8,128)S(1)} %broadcast_in_dim.101.clone, s32[16]{0:T(128)S(1)} %fusion.37, f32[16,32,1536]{2,1,0:T(8,128)} %reshape.282), kind=kCustom, calls=%fused_computation.4 | custom fusion | flops 786432 | bytes 9437248 | tf_op jit(solution)/shard_map/scatter-add | solution.py:133
  167.5 4.4 %all-to-all-start.2 = ((bf16[8,32,1536]{2,1,0:T(8,128)(2,1)}), bf16[8,32,1536]{2,1,0:T(8,128)(2,1)}, u32[]{:S(2)}, u32[]{:S(2)}) async-start(bf16[8,32,1536]{2,1,0:T(8,128)(2,1)} %convert_element_type.66), calls=%async_computation.2 | async-start | bytes 1572864 | tf_op jit(solution)/shard_map/all_to_all | solution.py:136
  172.5 8.0 %convolution_bitcast_fusion = f32[2,384,12,128]{1,3,2,0:T(8,128)} fusion(bf16[2,128,12,128]{1,3,2,0:T(8,128)(2,1)S(1)} %copy.85, f32[2,12,128]{2,1,0:T(8,128)S(1)} %get-tuple-element.34, f32[2,12,384,128]{3,2,1,0:T(8,128)} %copy-done), kind=kOutput, calls=%fused_computation.23 | convolution fusion | flops 307891584 | bytes 10235904 | tf_op jit(solution)/shard_map/chqk,cqhd->ckhd/dot_general | solution.py:124
  182.4 3.4 %copy.101 = f32[2,256,12,128]{3,2,1,0:T(8,128)} copy(f32[2,256,12,128]{1,3,2,0:T(8,128)S(1)} %slice-done.2) | data formatting | bytes 6291456 | tf_op jit(solution)/shard_map/slice | solution.py:130
  185.8 4.7 %reshape.290 = f32[16,32,1536]{2,1,0:T(8,128)} reshape(f32[2,256,12,128]{3,2,1,0:T(8,128)} %copy.101) | data formatting | bytes 6291456 | tf_op jit(solution)/shard_map/reshape | solution.py:130
  190.6 5.4 %scatter_fusion.1 = f32[8,32,1536]{2,1,0:T(8,128)S(1)} fusion(f32[8,32,1536]{2,1,0:T(8,128)S(1)} %broadcast_in_dim.101.clone.1, s32[16]{0:T(128)S(1)} %fusion.37, f32[16,32,1536]{2,1,0:T(8,128)} %reshape.290), kind=kCustom, calls=%fused_computation.5 | custom fusion | flops 786432 | bytes 9437248 | tf_op jit(solution)/shard_map/scatter-add | solution.py:134
  197.0 4.4 %all-to-all-start.3 = ((bf16[8,32,1536]{2,1,0:T(8,128)(2,1)}), bf16[8,32,1536]{2,1,0:T(8,128)(2,1)}, u32[]{:S(2)}, u32[]{:S(2)}) async-start(bf16[8,32,1536]{2,1,0:T(8,128)(2,1)} %convert_element_type.68), calls=%async_computation.3 | async-start | bytes 1572864 | tf_op jit(solution)/shard_map/all_to_all | solution.py:137
  224.5 13.9 %reduce-scatter.2.cloned.1.call-done = bf16[768,1536]{0,1:T(8,128)(2,1)} async-done(((bf16[3072,1536]{0,1:T(8,128)(2,1)}), bf16[768,1536]{0,1:T(8,128)(2,1)}) %reduce-scatter.2.cloned.1.call-update) | async-done | bytes 2359312 | tf_op jit(solution)/shard_map/reduce_scatter | solution.py:155
  238.4 4.6 %copy.106 = f32[768,1536]{1,0:T(8,128)} copy(bf16[768,1536]{0,1:T(8,128)(2,1)} %reduce-scatter.2.cloned.1.call-done) | data formatting | bytes 7077888
  (93 shorter events, 63.3 us)
Async XLA Ops:
  7.2 1.5 copy-start.10
  7.2 8.2 %copy-start.6 = (bf16[8,32,1536]{2,1,0:T(8,128)(2,1)S(1)}, bf16[8,32,1536]{2,1,0:T(8,128)(2,1)}, u32[]{:S(2)}) copy-start(bf16[8,32,1536]{2,1,0:T(8,128)(2,1)} %param.12) | copy-start | bytes 2359300
  7.2 102.5 %all-gather.4.cloned.1.call-start = ((), (), s32[]{:S(2)}) async-start(), calls=%async_computation.5 | async-start | bytes 2359296 | tf_op jit(solution)/shard_map/all_gather | solution.py:72
  7.9 8.1 %copy-start.5 = (bf16[8,32,1536]{2,1,0:T(8,128)(2,1)S(1)}, bf16[8,32,1536]{2,1,0:T(8,128)(2,1)}, u32[]{:S(2)}) copy-start(bf16[8,32,1536]{2,1,0:T(8,128)(2,1)} %param.11) | copy-start | bytes 2359300
  7.9 113.3 %all-gather.6.cloned.1.call-start = ((), (), s32[]{:S(2)}) async-start(), calls=%async_computation.6 | async-start | bytes 11796480 | tf_op jit(solution)/shard_map/all_gather | solution.py:77
  44.0 40.0 %all-to-all-start = ((bf16[16,32,1536]{2,1,0:T(8,128)(2,1)}), bf16[16,32,1536]{2,1,0:T(8,128)(2,1)}, u32[]{:S(2)}, u32[]{:S(2)}) async-start(bf16[16,32,1536]{2,1,0:T(8,128)(2,1)} %get-tuple-element.30), calls=%async_computation | async-start | bytes 3145728 | tf_op jit(solution)/shard_map/all_to_all | solution.py:64
  49.0 3.1 %copy-start.9 = (bf16[8,32,1536]{2,1,0:T(8,128)(2,1)S(1)}, bf16[8,32,1536]{2,1,0:T(8,128)(2,1)}, u32[]{:S(2)}) copy-start(bf16[8,32,1536]{2,1,0:T(8,128)(2,1)} %param.10) | copy-start | bytes 2359300
  49.0 189.4 %reduce-scatter.2.cloned.1.call-start = ((), (), s32[]{:S(2)}) async-start(), calls=%async_computation.7 | async-start | bytes 11796480 | tf_op jit(solution)/shard_map/reduce_scatter | solution.py:155
  52.6 1.7 copy-start.7
  99.0 2.3 copy-start.4
  101.2 2.8 %copy-start.2 = (bf16[2,384,12,128]{3,1,2,0:T(8,128)(2,1)}, bf16[2,384,12,128]{3,1,2,0:T(8,128)(2,1)S(1)}, u32[]{:S(2)}) copy-start(bf16[2,384,12,128]{3,1,2,0:T(8,128)(2,1)S(1)} %copy_dynamic-update-slice_fusion.1) | copy-start | bytes 7077892
  104.0 2.2 copy-start
  136.3 1.4 copy-start.8
  146.8 1.4 copy-start.3
  149.0 2.2 copy-start.1
  167.5 29.5 %all-to-all-start.2 = ((bf16[8,32,1536]{2,1,0:T(8,128)(2,1)}), bf16[8,32,1536]{2,1,0:T(8,128)(2,1)}, u32[]{:S(2)}, u32[]{:S(2)}) async-start(bf16[8,32,1536]{2,1,0:T(8,128)(2,1)} %convert_element_type.66), calls=%async_computation.2 | async-start | bytes 1572864 | tf_op jit(solution)/shard_map/all_to_all | solution.py:136
  180.5 1.9 slice-start.2
  197.0 24.0 %all-to-all-start.3 = ((bf16[8,32,1536]{2,1,0:T(8,128)(2,1)}), bf16[8,32,1536]{2,1,0:T(8,128)(2,1)}, u32[]{:S(2)}, u32[]{:S(2)}) async-start(bf16[8,32,1536]{2,1,0:T(8,128)(2,1)} %convert_element_type.68), calls=%async_computation.3 | async-start | bytes 1572864 | tf_op jit(solution)/shard_map/all_to_all | solution.py:137
  204.7 2.4 slice-start
  209.3 2.0 slice-start.1
Sparse Core Ops, SparseCore 0:
  9.6 29.2 all-gather.3
  40.4 80.7 all-gather.5
  142.9 95.4 reduce-scatter.1
where the time goes:
time: 251 us; the launch traced here: 249 us
  local copies, waits for them, and re-layouts  73.7 us (29%)
  waiting for transfers between devices  54.5 us (22%)
  matrix products  40.2 us (16%)
  blocking collectives  28.9 us (12%)
  other arithmetic  24.1 us (10%)
  between operations  14.1 us (6%)
  starting transfers between devices  13.9 us (6%)
    all_to_all x1, waiting for transfers between devices, per_device(): lax.all_to_all(pack_slots(keys, source, filled), 'tm', split_axis=0, conc...  25.2 us
    all_to_all x1, blocking collectives, per_device(): lax.all_to_all(pack_slots(values, source, filled), 'tm', split_axis=0, co...  23 us
    unnamed x27, local copies, waits for them, and re-layouts  16 us
    reduce_scatter x1, waiting for transfers between devices, per_device(): lax.psum_scatter(lax.dot_general(columns, attn_rows, (((0,), (0,)), ((),...  13.9 us
    all_gather x1, waiting for transfers between devices, per_device(): lax.all_gather(out_weight, 'tm', axis=0, tiled=True)  11.5 us
    dot_general x1, matrix products, per_device(): jnp.einsum('chqk,cqhd->ckhd', prob_low, grad_blocks, preferred_element_ty...  7.96 us
    dot_general x1, matrix products, per_device(): jnp.einsum('chqk,ckhd->cqhd', prob_low, value_set, preferred_element_type...  6.99 us
    dot_general x1, matrix products, per_device(): jnp.dot(columns, lax.all_gather(out_weight, 'tm', axis=0, tiled=True), pr...  6.76 us
  transfers between devices with their start and end apart: 6, of which 4 were waited for; matrix products, arithmetic and copies ran while one was open for 42% of the time, Pallas kernels for 0%

commit v1 on v0

--- a/solution.py
+++ b/solution.py
@@ -1,6 +1,10 @@
+import functools
+
 import jax
 import jax.numpy as jnp
 from jax import lax
+from jax.experimental import pallas as pl
+from jax.experimental.pallas import tpu as pltpu
 from jax.sharding import PartitionSpec as P
 
 HD = 128
@@ -163,9 +167,355 @@
     return (query_grad.reshape(frames_dev, frame_tokens, width), key_grad, value_grad, weight_grad)
 
 
+SELF, MATE, PARTNER, DIAG = 0, 1, 2, 3
+F32 = jnp.float32
+BF16 = jnp.bfloat16
+NT = (((1,), (1,)), ((), ()))
+TN = (((0,), (0,)), ((), ()))
+
+
+def dot(a, b):
+    return jnp.dot(a, b, preferred_element_type=F32)
+
+
+def dotx(a, b, dims):
+    return lax.dot_general(a, b, dims, preferred_element_type=F32)
+
+
+def fused_kernel(
+    slots, q_ref, k_ref, v_ref, og_ref, w_ref, lists_ref,
+    dq_ref, dk_ref, dv_ref, dw_ref,
+    every_list, present, pick, send_k, send_v, far_k, far_v, og_halves, columns, columns_t,
+    part_a, part_b, mate_out, mate_in, pair_out, pair_in, grad, attn, prob,
+    own_k, own_v, back_k, back_v, came_k, came_v, send_sem, recv_sem,
+):
+    rows, width = q_ref.shape
+    heads = width // HD
+    entries = lists_ref.shape[0]
+    frame_tokens = 32
+    group_rows = CF * frame_tokens
+    groups = rows // group_rows
+    far_rows = slots * frame_tokens
+    depth = w_ref.shape[0]
+    scale = HD ** (-0.5)
+    t = lax.axis_index("tm")
+    h = lax.axis_index("head")
+    mate = t + 1 - 2 * (t % 2)
+    partner = (t + 2) % 4
+    diag = (mate + 2) % 4
+    peers = (t, mate, partner, diag)
+
+    barrier = pltpu.get_barrier_semaphore()
+    for kind in (MATE, PARTNER, DIAG):
+        pl.semaphore_signal(barrier, inc=1, device_id={"tm": peers[kind]})
+    pl.semaphore_signal(barrier, inc=1, device_id={"head": 1 - h})
+    pl.semaphore_wait(barrier, 4)
+
+    started = []
+
+    def send(src, dst, target):
+        number = len(started)
+        copy = pltpu.make_async_remote_copy(
+            src_ref=src, dst_ref=dst, send_sem=send_sem.at[number], recv_sem=recv_sem.at[number],
+            device_id=target,
+        )
+        copy.start()
+        started.append(copy)
+        return copy
+
+    def to(kind):
+        return {"tm": peers[kind]}
+
+    lists_in = [
+        send(lists_ref, every_list.at[kind], to(kind)) for kind in (PARTNER, DIAG, MATE)
+    ]
+    halves_in = []
+    for part in range(2):
+        og_halves[h, part] = og_ref[:, part * depth : (part + 1) * depth]
+    for part in range(2):
+        halves_in.append(
+            send(og_halves.at[h, part], og_halves.at[h, part], {"head": 1 - h})
+        )
+    every_list[SELF] = lists_ref[...]
+    for copy in lists_in:
+        copy.wait_recv()
+
+    lanes = lax.broadcasted_iota(jnp.int32, (entries, rows), 1)
+    my_frame = t * (rows // frame_tokens) + lax.shift_right_logical(lanes, 5)
+    for kind in range(4):
+        named = jnp.max((every_list[kind] == my_frame).astype(F32), axis=0, keepdims=True)
+        present[kind * frame_tokens : (kind + 1) * frame_tokens, :] = jnp.broadcast_to(
+            named, (frame_tokens, rows)
+        ).astype(BF16)
+    above = lax.broadcasted_iota(jnp.int32, (rows, rows), 0)
+    below = lax.broadcasted_iota(jnp.int32, (rows, rows), 1)
+    earlier = (
+        ((above & 31) == 0)
+        & (lax.shift_right_logical(above, 5) < lax.shift_right_logical(below, 5))
+    ).astype(F32).astype(BF16)
+    rank = dot(present[...], earlier)
+    token = lax.broadcasted_iota(jnp.int32, (frame_tokens, rows), 0)
+    column_token = lax.broadcasted_iota(jnp.int32, (frame_tokens, rows), 1) & 31
+    same_token = (token == column_token).astype(F32)
+    for kind in range(4):
+        span = slice(kind * frame_tokens, (kind + 1) * frame_tokens)
+        here = present[span, :].astype(F32) * same_token
+        for slot in range(slots):
+            first = (kind * slots + slot) * frame_tokens
+            pick[first : first + frame_tokens, :] = (
+                here * (rank[span, :] == slot).astype(F32)
+            ).astype(BF16)
+
+    tile = 512
+
+    def tiled(body):
+        def step(i, carry):
+            body(pl.ds(pl.multiple_of(i * tile, tile), tile))
+            return carry
+
+        lax.fori_loop(0, width // tile, step, 0)
+
+    def span_of(kind):
+        return pl.ds(kind * far_rows, far_rows)
+
+    def pick_keys(cols):
+        send_k[:, cols] = dot(pick[...], k_ref[:, cols]).astype(BF16)
+
+    def pick_values(cols):
+        send_v[:, cols] = dot(pick[...], v_ref[:, cols]).astype(BF16)
+
+    frames_in = []
+    tiled(pick_keys)
+    for kind in (PARTNER, DIAG, MATE):
+        frames_in.append(send(send_k.at[span_of(kind)], far_k.at[span_of(kind)], to(kind)))
+    tiled(pick_values)
+    for kind in (PARTNER, DIAG, MATE):
+        frames_in.append(send(send_v.at[span_of(kind)], far_v.at[span_of(kind)], to(kind)))
+    far_k[0:far_rows, :] = send_k[0:far_rows, :]
+    far_v[0:far_rows, :] = send_v[0:far_rows, :]
+
+    for copy in halves_in:
+        copy.wait_recv()
+    columns_in = {}
+    for kind in (PARTNER, DIAG, MATE):
+        peer = peers[kind]
+        columns_in[kind] = send(
+            og_halves.at[peer // 2, peer % 2], columns.at[pl.ds(kind * rows, rows)], to(kind)
+        )
+    columns[0:rows, :] = og_halves[t // 2, t % 2]
+
+    for copy in frames_in:
+        copy.wait_recv()
+
+    def forward(i, carry):
+        cols = pl.ds(pl.multiple_of(i * HD, HD), HD)
+        fk = far_k[:, cols]
+        fv = far_v[:, cols]
+        for g in range(groups):
+            span = slice(g * group_rows, (g + 1) * group_rows)
+            q = q_ref[span, cols]
+            near = dotx(q, k_ref[span, cols], NT) * scale
+            far = dotx(q, fk, NT) * scale
+            top = jnp.maximum(
+                jnp.max(near, axis=1, keepdims=True), jnp.max(far, axis=1, keepdims=True)
+            )
+            near = jnp.exp(near - top)
+            far = jnp.exp(far - top)
+            total = jnp.sum(near, axis=1, keepdims=True) + jnp.sum(far, axis=1, keepdims=True)
+            near = near / total
+            far = far / total
+            prob[i, span, 0:group_rows] = near
+            prob[i, span, group_rows:] = far
+            out = dot(near.astype(BF16), v_ref[span, cols]) + dot(far.astype(BF16), fv)
+            attn[span, cols] = out.astype(BF16)
+        return carry
+
+    lax.fori_loop(0, heads, forward, 0)
+    own = attn.at[pl.ds(0, rows)]
+    attn_partner = send(own, attn.at[pl.ds(PARTNER * rows, rows)], to(PARTNER))
+    attn_mate = send(own, attn.at[pl.ds(MATE * rows, rows)], to(MATE))
+
+    def block(kind):
+        return slice(kind * rows, (kind + 1) * rows)
+
+    columns_in[DIAG].wait_recv()
+
+    def diag_part(cols):
+        mate_out[1, :, cols] = dot(columns[block(DIAG), :], w_ref[:, cols]).astype(BF16)
+
+    tiled(diag_part)
+    diag_in = send(mate_out.at[1], mate_in.at[1], to(MATE))
+    columns_in[PARTNER].wait_recv()
+
+    def partner_part(cols):
+        part_b[:, cols] = dot(columns[block(PARTNER), :], w_ref[:, cols])
+
+    tiled(partner_part)
+    diag_in.wait_recv()
+
+    def pair_sum(cols):
+        pair_out[:, cols] = (part_b[:, cols] + mate_in[1, :, cols].astype(F32)).astype(BF16)
+
+    tiled(pair_sum)
+    pair = send(pair_out, pair_in, to(PARTNER))
+    columns_in[MATE].wait_recv()
+
+    def mate_part(cols):
+        mate_out[0, :, cols] = dot(columns[block(MATE), :], w_ref[:, cols]).astype(BF16)
+
+    tiled(mate_part)
+    mate_sum = send(mate_out.at[0], mate_in.at[0], to(MATE))
+
+    def own_part(cols):
+        part_a[:, cols] = dot(columns[block(SELF), :], w_ref[:, cols])
+
+    tiled(own_part)
+    attn_partner.wait_recv()
+    held = attn.at[pl.ds(PARTNER * rows, rows)]
+    attn_diag = send(held, attn.at[pl.ds(DIAG * rows, rows)], to(MATE))
+    for kind in range(4):
+        columns_t[:, block(kind)] = columns[block(kind), :].T
+    mate_sum.wait_recv()
+    pair.wait_recv()
+
+    def total_part(cols):
+        grad[:, cols] = (
+            part_a[:, cols] + mate_in[0, :, cols].astype(F32) + pair_in[:, cols].astype(F32)
+        ).astype(BF16)
+
+    tiled(total_part)
+
+    def backward(i, carry):
+        cols = pl.ds(pl.multiple_of(i * HD, HD), HD)
+        fk = far_k[:, cols]
+        fv = far_v[:, cols]
+        far_dk = None
+        far_dv = None
+        for g in range(groups):
+            span = slice(g * group_rows, (g + 1) * group_rows)
+            q = q_ref[span, cols]
+            do = grad[span, cols]
+            row_dot = jnp.sum(
+                do.astype(F32) * attn[span, cols].astype(F32), axis=1, keepdims=True
+            )
+            near = prob[i, span, 0:group_rows]
+            far = prob[i, span, group_rows:]
+            near_ds = (near * (dotx(do, v_ref[span, cols], NT) - row_dot)).astype(BF16)
+            far_ds = (far * (dotx(do, fv, NT) - row_dot)).astype(BF16)
+            near_p = near.astype(BF16)
+            far_p = far.astype(BF16)
+            dq_ref[span, cols] = (
+                (dot(near_ds, k_ref[span, cols]) + dot(far_ds, fk)) * scale
+            ).astype(BF16)
+            own_k[span, cols] = dotx(near_ds, q, TN) * scale
+            own_v[span, cols] = dotx(near_p, do, TN)
+            more_k = dotx(far_ds, q, TN)
+            more_v = dotx(far_p, do, TN)
+            far_dk = more_k if g == 0 else far_dk + more_k
+            far_dv = more_v if g == 0 else far_dv + more_v
+        back_k[:, cols] = (far_dk * scale).astype(BF16)
+        back_v[:, cols] = far_dv.astype(BF16)
+        return carry
+
+    returned = []
+    chunks = 2
+    for chunk in range(chunks):
+        each = heads // chunks
+        lax.fori_loop(chunk * each, (chunk + 1) * each, backward, 0)
+        cols = pl.ds(chunk * each * HD, each * HD)
+        for kind in (PARTNER, DIAG, MATE):
+            for out, into in ((back_k, came_k), (back_v, came_v)):
+                returned.append(
+                    send(out.at[span_of(kind), cols], into.at[span_of(kind), cols], to(kind))
+                )
+    came_k[0:far_rows, :] = back_k[0:far_rows, :]
+    came_v[0:far_rows, :] = back_v[0:far_rows, :]
+    attn_mate.wait_recv()
+    attn_diag.wait_recv()
+
+    def weight_part(cols):
+        dw_ref[:, cols] = dot(columns_t[...], attn[:, cols])
+
+    tiled(weight_part)
+    for copy in returned:
+        copy.wait_recv()
+
+    def add_returned(cols):
+        dk_ref[:, cols] = (own_k[:, cols] + dotx(pick[...], came_k[:, cols], TN)).astype(BF16)
+        dv_ref[:, cols] = (own_v[:, cols] + dotx(pick[...], came_v[:, cols], TN)).astype(BF16)
+
+    tiled(add_returned)
+    for copy in started:
+        copy.wait_send()
+
+
+def fused(queries, keys, values, out_grad, out_weight, lists):
+    frames, frame_tokens, width = queries.shape
+    rows = frames * frame_tokens
+    depth = out_weight.shape[0]
+    slots = RET // 4
+    heads = width // HD
+    flat = [x.reshape(rows, width) for x in (queries, keys, values, out_grad)]
+    spread = jnp.broadcast_to(lists.reshape(-1, 1), (lists.size, rows))
+    vmem = pl.BlockSpec(memory_space=pltpu.VMEM)
+    far = 4 * slots * frame_tokens
+
+    def low(*shape):
+        return pltpu.VMEM(shape, BF16)
+
+    def wide(*shape):
+        return pltpu.VMEM(shape, F32)
+
+    dq, dk, dv, dw = pl.pallas_call(
+        functools.partial(fused_kernel, slots),
+        out_shape=[jax.ShapeDtypeStruct((rows, width), BF16)] * 3
+        + [jax.ShapeDtypeStruct((depth, width), F32)],
+        in_specs=[vmem] * 6,
+        out_specs=[vmem] * 4,
+        scratch_shapes=[
+            pltpu.VMEM((4, lists.size, rows), jnp.int32),
+            low(4 * frame_tokens, rows),
+            low(far, rows),
+            low(far, width),
+            low(far, width),
+            low(far, width),
+            low(far, width),
+            low(2, 2, rows, depth),
+            low(4 * rows, depth),
+            low(depth, 4 * rows),
+            wide(rows, width),
+            wide(rows, width),
+            low(2, rows, width),
+            low(2, rows, width),
+            low(rows, width),
+            low(rows, width),
+            low(rows, width),
+            low(4 * rows, width),
+            wide(heads, rows, CF * frame_tokens + far),
+            wide(rows, width),
+            wide(rows, width),
+            low(far, width),
+            low(far, width),
+            low(far, width),
+            low(far, width),
+            pltpu.SemaphoreType.DMA((48,)),
+            pltpu.SemaphoreType.DMA((48,)),
+        ],
+        compiler_params=pltpu.CompilerParams(
+            collective_id=0, has_side_effects=True, vmem_limit_bytes=60 * 1024 * 1024
+        ),
+        cost_estimate=pl.CostEstimate(
+            flops=7 * 10**9, bytes_accessed=16 * 10**6, transcendentals=10**6
+        ),
+    )(*flat, out_weight, spread)
+    back = [x.reshape(frames, frame_tokens, width) for x in (dq, dk, dv)]
+    return (*back, dw)
+
+
 def solution(mesh):
+    whole_fits = mesh.shape["tm"] == 4 and mesh.shape["head"] == 2
     return jax.shard_map(
-        per_device,
+        fused if whole_fits else per_device,
         mesh=mesh,
         in_specs=(
             P(("dp", "tm"), None, "head"),

time: 251 us -> 117 us (0.47)
  Pallas kernels: 0 us -> 106 us
  local copies, waits for them, and re-layouts: 73.7 us -> 9.97 us
  waiting for transfers between devices: 54.5 us -> 0 us
  matrix products: 40.2 us -> 0 us
  blocking collectives: 28.9 us -> 0 us
  other arithmetic: 24.1 us -> 0 us
  starting transfers between devices: 13.9 us -> 0 us
  between operations: 14.1 us -> 0.65 us
    pallas_call x0 -> x1, Pallas kernels: none -> 106 us  [fused(): pl.pallas_call(functools.partial(fused_kernel, slots), out_shape=[jax.Sha...]
    dot_general x10 -> x0, matrix products: 40.2 us -> none  [the longest x1 7.96 us: per_device(): jnp.einsum('chqk,cqhd->ckhd', prob_low, grad_blocks, preferred_element_ty...]
    reshape x14 -> x0, local copies, waits for them, and re-layouts: 27.7 us -> none  [the longest x1 5.15 us: per_device(): far_dk = key_term[:, group_rows:].reshape(entry_count, frame_tokens, width)]
    all_to_all x3 -> x0, waiting for transfers between devices: 27.7 us -> none  [the longest x1 25.2 us: per_device(): lax.all_to_all(pack_slots(keys, source, filled), 'tm', split_axis=0, conc...]
    all_to_all x1 -> x0, blocking collectives: 23 us -> none  [per_device(): lax.all_to_all(pack_slots(values, source, filled), 'tm', split_axis=0, co...]
    slice x11 -> x0, local copies, waits for them, and re-layouts: 14.4 us -> none  [the longest x3 5.29 us: per_device(): value_term[:, group_rows:].reshape(entry_count, frame_tokens, width)]
    reduce_scatter x1 -> x0, waiting for transfers between devices: 13.9 us -> none  [per_device(): lax.psum_scatter(lax.dot_general(columns, attn_rows, (((0,), (0,)), ((),...]
    all_to_all x3 -> x0, starting transfers between devices: 13.8 us -> none  [the longest x1 5.01 us: per_device(): lax.all_to_all(pack_slots(keys, source, filled), 'tm', split_axis=0, conc...]
  transfers between devices with their start and end apart: 6 -> 0, of which waited for: 4 -> 0; matrix products, arithmetic and copies ran while one was open for 42% -> 0% of each run, Pallas kernels for 0% -> 0%
where the time goes in v1:
time: 117 us
  Pallas kernels  106 us (91%)
  local copies, waits for them, and re-layouts  9.97 us (9%)
    pallas_call x1, Pallas kernels, fused(): pl.pallas_call(functools.partial(fused_kernel, slots), out_shape=[jax.Sha...  106 us
    unnamed x6, local copies, waits for them, and re-layouts  8.53 us

profile of v1, /device:TPU:1, one launch (start us, length us, event | category | flops | bytes accessed | tf_op | source)
XLA Modules:
  0.0 116.6 jit_solution(17113727091567392265)
XLA Ops:
  0.6 0.8 broadcast_in_dim.7
  1.4 0.7 broadcast_in_dim.8.lists_ref
  2.1 106.0 %shard_map.93 = (bf16[256,1536]{1,0:T(8,128)(2,1)}, bf16[256,1536]{1,0:T(8,128)(2,1)}, bf16[256,1536]{1,0:T(8,128)(2,1)}, f32[768,1536]{1,0:T(8,128)}) custom-call(bf16[256,1536]{1,0:T(8,128)(2,1)} %bitcast.10, bf16[256,1536]{1,0:T(8,128)(2,1)} %bitcast.11, bf16[256,1536]{1,0:T(8,128)(2,1)} %bitcast.12, bf16[256,1536]{1,0:T(8,128)(2,1)} %bitcast.13, ...), custom_call_target="tpu_custom_call" | custom-call | flops 7000000000 | bytes 16000000 | tf_op jit(solution)/shard_map/pallas_call | solution.py:469
  108.1 0.0 copy-start
  108.1 2.2 %copy.14 = bf16[8,32,1536]{2,1,0:T(8,128)(2,1)} copy(bf16[8,32,1536]{2,1,0:T(8,128)(2,1)} %bitcast.9) | data formatting | bytes 1572864
  110.3 2.1 %copy.15 = bf16[8,32,1536]{2,1,0:T(8,128)(2,1)} copy(bf16[8,32,1536]{2,1,0:T(8,128)(2,1)} %bitcast.8) | data formatting | bytes 1572864
  112.4 2.1 %copy.16 = bf16[8,32,1536]{2,1,0:T(8,128)(2,1)} copy(bf16[8,32,1536]{2,1,0:T(8,128)(2,1)} %bitcast.7) | data formatting | bytes 1572864
  114.4 0.0 copy-done
  114.4 2.2 %copy.17 = f32[768,1536]{1,0:T(8,128)} copy(f32[768,1536]{1,0:T(8,128)S(1)} %copy-done) | data formatting | bytes 9437184
Async XLA Ops:
  108.1 6.4 %copy-start = (f32[768,1536]{1,0:T(8,128)S(1)}, f32[768,1536]{1,0:T(8,128)}, u32[]{:S(2)}) copy-start(f32[768,1536]{1,0:T(8,128)} %get-tuple-element.19) | copy-start | bytes 14155780

commit v2 on v1

--- a/solution.py
+++ b/solution.py
@@ -183,23 +183,29 @@
 
 
 def fused_kernel(
-    slots, q_ref, k_ref, v_ref, og_ref, w_ref, lists_ref,
+    slots, line, lists_ref, q_ref, k_ref, v_ref, og_ref, w_ref,
     dq_ref, dk_ref, dv_ref, dw_ref,
-    every_list, present, pick, send_k, send_v, far_k, far_v, og_halves, columns, columns_t,
-    part_a, part_b, mate_out, mate_in, pair_out, pair_in, grad, attn, prob,
-    own_k, own_v, back_k, back_v, came_k, came_v, send_sem, recv_sem,
+    my_list, every_list, present, pick, send_k, send_v, far_k, far_v, og_halves, columns,
+    columns_t, w_in, grad, attn, prob,
+    own_k, own_v, back_k, back_v, came_k, came_v,
+    send_sem, recv_sem, up_send, up_recv, down_send, down_recv,
 ):
     rows, width = q_ref.shape
     heads = width // HD
-    entries = lists_ref.shape[0]
+    entries = my_list.shape[0]
     frame_tokens = 32
     group_rows = CF * frame_tokens
     groups = rows // group_rows
     far_rows = slots * frame_tokens
     depth = w_ref.shape[0]
+    chunks = 2
+    span_width = width // chunks
+    piece = depth // line
+    half_rows = rows // 2
     scale = HD ** (-0.5)
     t = lax.axis_index("tm")
     h = lax.axis_index("head")
+    z = lax.axis_index("dp")
     mate = t + 1 - 2 * (t % 2)
     partner = (t + 2) % 4
     diag = (mate + 2) % 4
@@ -209,7 +215,15 @@
     for kind in (MATE, PARTNER, DIAG):
         pl.semaphore_signal(barrier, inc=1, device_id={"tm": peers[kind]})
     pl.semaphore_signal(barrier, inc=1, device_id={"head": 1 - h})
-    pl.semaphore_wait(barrier, 4)
+
+    for move in (1, line - 1):
+        pl.semaphore_signal(barrier, inc=1, device_id={"dp": (z + move) % line})
+
+    for entry in range(entries):
+        named = lists_ref[entry // RET, entry % RET]
+        my_list[entry : entry + 1, :] = jnp.full((1, rows), named, jnp.int32)
+        every_list[SELF, entry : entry + 1, :] = jnp.full((1, rows), named, jnp.int32)
+    pl.semaphore_wait(barrier, 6)
 
     started = []
 
@@ -227,8 +241,68 @@
         return {"tm": peers[kind]}
 
     lists_in = [
-        send(lists_ref, every_list.at[kind], to(kind)) for kind in (PARTNER, DIAG, MATE)
+        send(my_list, every_list.at[kind], to(kind)) for kind in (PARTNER, DIAG, MATE)
     ]
+
+    def chunk_cols(chunk):
+        return pl.ds(chunk * span_width, span_width)
+
+    def piece_rows(index):
+        return pl.ds(pl.multiple_of(index * piece, piece), piece)
+
+    crossing = []
+    for chunk in range(chunks):
+        crossing.append(
+            send(
+                w_ref.at[piece_rows(z), chunk_cols(chunk)],
+                w_in.at[PARTNER, chunk, piece_rows(z)],
+                to(PARTNER),
+            )
+        )
+    mate_w = [
+        send(w_ref.at[:, chunk_cols(chunk)], w_in.at[MATE, chunk], to(MATE))
+        for chunk in range(chunks)
+    ]
+
+    def hop(chunk, step, upward):
+        move = 1 if upward else -1
+        index = z - step if upward else z + step
+        index = jnp.clip(index, 0, line - 1)
+        held = w_in.at[PARTNER, chunk, piece_rows(index)]
+        sends, recvs = (up_send, up_recv) if upward else (down_send, down_recv)
+        return pltpu.make_async_remote_copy(
+            src_ref=held, dst_ref=held, send_sem=sends.at[chunk, step],
+            recv_sem=recvs.at[chunk, step], device_id={"dp": z + move},
+        )
+
+    def hop_sent(step, upward):
+        if upward:
+            return (z - step >= 0) & (z < line - 1)
+        return (z + step < line) & (z > 0)
+
+    def hop_received(step, upward):
+        if upward:
+            return z - 1 - step >= 0
+        return z + 1 + step < line
+
+    def hop_wait(chunk, step):
+        for upward in (True, False):
+
+            @pl.when(hop_received(step, upward))
+            def arrived():
+                hop(chunk, step, upward).wait_recv()
+
+    def hop_start(chunk, step):
+        if step == 0:
+            crossing[chunk].wait_recv()
+        else:
+            hop_wait(chunk, step - 1)
+        for upward in (True, False):
+
+            @pl.when(hop_sent(step, upward))
+            def onward():
+                hop(chunk, step, upward).start()
+
     halves_in = []
     for part in range(2):
         og_halves[h, part] = og_ref[:, part * depth : (part + 1) * depth]
@@ -236,7 +310,6 @@
         halves_in.append(
             send(og_halves.at[h, part], og_halves.at[h, part], {"head": 1 - h})
         )
-    every_list[SELF] = lists_ref[...]
     for copy in lists_in:
         copy.wait_recv()
 
@@ -294,15 +367,23 @@
     far_k[0:far_rows, :] = send_k[0:far_rows, :]
     far_v[0:far_rows, :] = send_v[0:far_rows, :]
 
+
+    hop_start(0, 0)
+    hop_start(0, 1)
     for copy in halves_in:
         copy.wait_recv()
+    mine = pl.ds(pl.multiple_of(h * half_rows, half_rows), half_rows)
     columns_in = {}
-    for kind in (PARTNER, DIAG, MATE):
+    for kind in (PARTNER, DIAG):
         peer = peers[kind]
         columns_in[kind] = send(
-            og_halves.at[peer // 2, peer % 2], columns.at[pl.ds(kind * rows, rows)], to(kind)
+            og_halves.at[peer // 2, peer % 2, mine], columns.at[kind, mine], to(kind)
         )
-    columns[0:rows, :] = og_halves[t // 2, t % 2]
+    columns_in[MATE] = send(og_halves.at[mate // 2, mate % 2], columns.at[MATE], to(MATE))
+    columns[SELF] = og_halves[t // 2, t % 2]
+    hop_start(0, 2)
+    hop_start(1, 0)
+    hop_start(1, 1)
 
     for copy in frames_in:
         copy.wait_recv()
@@ -327,63 +408,25 @@
             prob[i, span, 0:group_rows] = near
             prob[i, span, group_rows:] = far
             out = dot(near.astype(BF16), v_ref[span, cols]) + dot(far.astype(BF16), fv)
-            attn[span, cols] = out.astype(BF16)
+            attn[SELF, span, cols] = out.astype(BF16)
         return carry
 
-    lax.fori_loop(0, heads, forward, 0)
-    own = attn.at[pl.ds(0, rows)]
-    attn_partner = send(own, attn.at[pl.ds(PARTNER * rows, rows)], to(PARTNER))
-    attn_mate = send(own, attn.at[pl.ds(MATE * rows, rows)], to(MATE))
-
-    def block(kind):
-        return slice(kind * rows, (kind + 1) * rows)
-
-    columns_in[DIAG].wait_recv()
-
-    def diag_part(cols):
-        mate_out[1, :, cols] = dot(columns[block(DIAG), :], w_ref[:, cols]).astype(BF16)
-
-    tiled(diag_part)
-    diag_in = send(mate_out.at[1], mate_in.at[1], to(MATE))
-    columns_in[PARTNER].wait_recv()
-
-    def partner_part(cols):
-        part_b[:, cols] = dot(columns[block(PARTNER), :], w_ref[:, cols])
-
-    tiled(partner_part)
-    diag_in.wait_recv()
-
-    def pair_sum(cols):
-        pair_out[:, cols] = (part_b[:, cols] + mate_in[1, :, cols].astype(F32)).astype(BF16)
-
-    tiled(pair_sum)
-    pair = send(pair_out, pair_in, to(PARTNER))
-    columns_in[MATE].wait_recv()
-
-    def mate_part(cols):
-        mate_out[0, :, cols] = dot(columns[block(MATE), :], w_ref[:, cols]).astype(BF16)
-
-    tiled(mate_part)
-    mate_sum = send(mate_out.at[0], mate_in.at[0], to(MATE))
-
-    def own_part(cols):
-        part_a[:, cols] = dot(columns[block(SELF), :], w_ref[:, cols])
-
-    tiled(own_part)
-    attn_partner.wait_recv()
-    held = attn.at[pl.ds(PARTNER * rows, rows)]
-    attn_diag = send(held, attn.at[pl.ds(DIAG * rows, rows)], to(MATE))
-    for kind in range(4):
-        columns_t[:, block(kind)] = columns[block(kind), :].T
-    mate_sum.wait_recv()
-    pair.wait_recv()
-
-    def total_part(cols):
-        grad[:, cols] = (
-            part_a[:, cols] + mate_in[0, :, cols].astype(F32) + pair_in[:, cols].astype(F32)
-        ).astype(BF16)
-
-    tiled(total_part)
+    each = heads // chunks
+    attn_partner = []
+    attn_mate = []
+    for chunk in range(chunks):
+        lax.fori_loop(chunk * each, (chunk + 1) * each, forward, 0)
+        own = attn.at[SELF, :, chunk_cols(chunk)]
+        attn_mate.append(send(own, attn.at[MATE, :, chunk_cols(chunk)], to(MATE)))
+        attn_partner.append(send(own, attn.at[PARTNER, :, chunk_cols(chunk)], to(PARTNER)))
+        if chunk == 0:
+            hop_start(1, 2)
+            hop_wait(0, 2)
+            diag_w = [send(w_in.at[PARTNER, 0], w_in.at[DIAG, 0], to(MATE))]
+    swapped = []
+    for kind in (PARTNER, DIAG):
+        columns_in[kind].wait_recv()
+        swapped.append(send(columns.at[kind, mine], columns.at[kind, mine], {"head": 1 - h}))
 
     def backward(i, carry):
         cols = pl.ds(pl.multiple_of(i * HD, HD), HD)
@@ -396,7 +439,7 @@
             q = q_ref[span, cols]
             do = grad[span, cols]
             row_dot = jnp.sum(
-                do.astype(F32) * attn[span, cols].astype(F32), axis=1, keepdims=True
+                do.astype(F32) * attn[SELF, span, cols].astype(F32), axis=1, keepdims=True
             )
             near = prob[i, span, 0:group_rows]
             far = prob[i, span, group_rows:]
@@ -418,11 +461,29 @@
         return carry
 
     returned = []
-    chunks = 2
+    step_width = 384
     for chunk in range(chunks):
-        each = heads // chunks
+        if chunk == 1:
+            hop_wait(1, 2)
+            diag_w.append(send(w_in.at[PARTNER, 1], w_in.at[DIAG, 1], to(MATE)))
+        mate_w[chunk].wait_recv()
+        diag_w[chunk].wait_recv()
+
+        def project(i, carry):
+            local = pl.ds(pl.multiple_of(i * step_width, step_width), step_width)
+            there = pl.ds(
+                pl.multiple_of(chunk * span_width + i * step_width, step_width), step_width
+            )
+            total = dot(og_halves[t // 2, t % 2], w_ref[:, there])
+            for kind in (MATE, PARTNER, DIAG):
+                peer = peers[kind]
+                total += dot(og_halves[peer // 2, peer % 2], w_in[kind, chunk, :, local])
+            grad[:, there] = total.astype(BF16)
+            return carry
+
+        lax.fori_loop(0, span_width // step_width, project, 0)
         lax.fori_loop(chunk * each, (chunk + 1) * each, backward, 0)
-        cols = pl.ds(chunk * each * HD, each * HD)
+        cols = chunk_cols(chunk)
         for kind in (PARTNER, DIAG, MATE):
             for out, into in ((back_k, came_k), (back_v, came_v)):
                 returned.append(
@@ -430,11 +491,24 @@
                 )
     came_k[0:far_rows, :] = back_k[0:far_rows, :]
     came_v[0:far_rows, :] = back_v[0:far_rows, :]
-    attn_mate.wait_recv()
-    attn_diag.wait_recv()
+    attn_diag = []
+    for chunk in range(chunks):
+        attn_partner[chunk].wait_recv()
+        held = attn.at[PARTNER, :, chunk_cols(chunk)]
+        attn_diag.append(send(held, attn.at[DIAG, :, chunk_cols(chunk)], to(MATE)))
+    columns_in[MATE].wait_recv()
+    for copy in swapped:
+        copy.wait_recv()
+    for kind in range(4):
+        columns_t[kind] = columns[kind].T
+    for copy in attn_mate + attn_diag:
+        copy.wait_recv()
 
     def weight_part(cols):
-        dw_ref[:, cols] = dot(columns_t[...], attn[:, cols])
+        total = dot(columns_t[SELF], attn[SELF, :, cols])
+        for kind in (MATE, PARTNER, DIAG):
+            total += dot(columns_t[kind], attn[kind, :, cols])
+        dw_ref[:, cols] = total.astype(BF16)
 
     tiled(weight_part)
     for copy in returned:
@@ -447,6 +521,38 @@
     tiled(add_returned)
     for copy in started:
         copy.wait_send()
+    for chunk in range(chunks):
+        for step in range(line - 1):
+            for upward in (True, False):
+
+                @pl.when(hop_sent(step, upward))
+                def left():
+                    hop(chunk, step, upward).wait_send()
+
+
+def finish_kernel(dq_ref, dk_ref, dv_ref, dw_ref, dq_out, dk_out, dv_out, dw_out):
+    dq_out[...] = dq_ref[...]
+    dk_out[...] = dk_ref[...]
+    dv_out[...] = dv_ref[...]
+    dw_out[...] = dw_ref[...].astype(F32)
+
+
+def finish(dq, dk, dv, dw):
+    steps = 4
+    rows, width = dq.shape
+    depth = dw.shape[0]
+    small = pl.BlockSpec((rows // steps, width), lambda i: (i, 0))
+    large = pl.BlockSpec((depth // steps, width), lambda i: (i, 0))
+    return pl.pallas_call(
+        finish_kernel,
+        grid=(steps,),
+        out_shape=[jax.ShapeDtypeStruct((rows, width), BF16)] * 3
+        + [jax.ShapeDtypeStruct((depth, width), F32)],
+        in_specs=[small, small, small, large],
+        out_specs=[small, small, small, large],
+        compiler_params=pltpu.CompilerParams(vmem_limit_bytes=32 * 1024 * 1024),
+        cost_estimate=pl.CostEstimate(flops=10**6, bytes_accessed=12 * 10**6, transcendentals=0),
+    )(dq, dk, dv, dw)
 
 
 def fused(queries, keys, values, out_grad, out_weight, lists):
@@ -456,7 +562,7 @@
     slots = RET // 4
     heads = width // HD
     flat = [x.reshape(rows, width) for x in (queries, keys, values, out_grad)]
-    spread = jnp.broadcast_to(lists.reshape(-1, 1), (lists.size, rows))
+    line = lax.axis_size("dp")
     vmem = pl.BlockSpec(memory_space=pltpu.VMEM)
     far = 4 * slots * frame_tokens
 
@@ -467,12 +573,13 @@
         return pltpu.VMEM(shape, F32)
 
     dq, dk, dv, dw = pl.pallas_call(
-        functools.partial(fused_kernel, slots),
+        functools.partial(fused_kernel, slots, line),
         out_shape=[jax.ShapeDtypeStruct((rows, width), BF16)] * 3
-        + [jax.ShapeDtypeStruct((depth, width), F32)],
-        in_specs=[vmem] * 6,
+        + [jax.ShapeDtypeStruct((depth, width), BF16)],
+        in_specs=[pl.BlockSpec(memory_space=pltpu.SMEM)] + [vmem] * 5,
         out_specs=[vmem] * 4,
         scratch_shapes=[
+            pltpu.VMEM((lists.size, rows), jnp.int32),
             pltpu.VMEM((4, lists.size, rows), jnp.int32),
             low(4 * frame_tokens, rows),
             low(far, rows),
@@ -481,16 +588,11 @@
             low(far, width),
             low(far, width),
             low(2, 2, rows, depth),
-            low(4 * rows, depth),
-            low(depth, 4 * rows),
-            wide(rows, width),
-            wide(rows, width),
-            low(2, rows, width),
-            low(2, rows, width),
+            low(4, rows, depth),
+            low(4, depth, rows),
+            low(4, 2, depth, width // 2),
             low(rows, width),
-            low(rows, width),
-            low(rows, width),
-            low(4 * rows, width),
+            low(4, rows, width),
             wide(heads, rows, CF * frame_tokens + far),
             wide(rows, width),
             wide(rows, width),
@@ -500,6 +602,10 @@
             low(far, width),
             pltpu.SemaphoreType.DMA((48,)),
             pltpu.SemaphoreType.DMA((48,)),
+            pltpu.SemaphoreType.DMA((2, line - 1)),
+            pltpu.SemaphoreType.DMA((2, line - 1)),
+            pltpu.SemaphoreType.DMA((2, line - 1)),
+            pltpu.SemaphoreType.DMA((2, line - 1)),
         ],
         compiler_params=pltpu.CompilerParams(
             collective_id=0, has_side_effects=True, vmem_limit_bytes=60 * 1024 * 1024
@@ -507,13 +613,14 @@
         cost_estimate=pl.CostEstimate(
             flops=7 * 10**9, bytes_accessed=16 * 10**6, transcendentals=10**6
         ),
-    )(*flat, out_weight, spread)
+    )(lists, *flat, out_weight)
+    dq, dk, dv, dw = finish(dq, dk, dv, dw)
     back = [x.reshape(frames, frame_tokens, width) for x in (dq, dk, dv)]
     return (*back, dw)
 
 
 def solution(mesh):
-    whole_fits = mesh.shape["tm"] == 4 and mesh.shape["head"] == 2
+    whole_fits = dict(mesh.shape) == {"dp": 4, "tm": 4, "head": 2}
     return jax.shard_map(
         fused if whole_fits else per_device,
         mesh=mesh,

time: 117 us -> 95.5 us (0.82); the launches traced: 117 us -> 93.7 us
  Pallas kernels: 106 us -> 88 us
  local copies, waits for them, and re-layouts: 9.97 us -> 5.06 us
    pallas_call x1 -> x2, Pallas kernels: 106 us -> 88 us  [the longest x1 84.8 us: fused(): pl.pallas_call(functools.partial(fused_kernel, slots, line), out_shape=[j...]
    unnamed x6 -> x8, local copies, waits for them, and re-layouts: 8.53 us -> 5.06 us
    broadcast_in_dim x2 -> x0, local copies, waits for them, and re-layouts: 1.44 us -> none  [fused(): spread = jnp.broadcast_to(lists.reshape(-1, 1), (lists.size, rows))]
where the time goes in v2:
time: 95.5 us; the launch traced here: 93.7 us
  Pallas kernels  88 us (92%)
  local copies, waits for them, and re-layouts  5.06 us (5%)
    pallas_call x1, Pallas kernels, fused(): pl.pallas_call(functools.partial(fused_kernel, slots, line), out_shape=[j...  84.8 us
    unnamed x8, local copies, waits for them, and re-layouts  5.06 us
    pallas_call x1, Pallas kernels, finish(): pl.pallas_call(finish_kernel, grid=(steps,), out_shape=[jax.ShapeDtypeStr...  3.15 us

profile of v2, /device:TPU:1, one launch (start us, length us, event | category | flops | bytes accessed | tf_op | source)
XLA Modules:
  0.0 93.7 jit_solution(11921015397993012378)
XLA Ops:
  0.6 84.8 %shard_map.93 = (bf16[256,1536]{1,0:T(8,128)(2,1)}, bf16[256,1536]{1,0:T(8,128)(2,1)}, bf16[256,1536]{1,0:T(8,128)(2,1)}, bf16[768,1536]{1,0:T(8,128)(2,1)}) custom-call(s32[2,8]{1,0:T(2,128)} %lists_ref.1, bf16[256,1536]{1,0:T(8,128)(2,1)} %bitcast.7, bf16[256,1536]{1,0:T(8,128)(2,1)} %bitcast.8, bf16[256,1536]{1,0:T(8,128)(2,1)} %bitcast.9, ...), custom_call_target="tpu_custom_call" | custom-call | flops 7000000000 | bytes 16000000 | tf_op jit(solution)/shard_map/pallas_call | solution.py:575
  85.5 0.0 copy-start
  85.5 1.7 %copy-done = bf16[768,1536]{1,0:T(8,128)(2,1)S(1)} copy-done((bf16[768,1536]{1,0:T(8,128)(2,1)S(1)}, bf16[768,1536]{1,0:T(8,128)(2,1)}, u32[]{:S(2)}) %copy-start) | copy-done | bytes 2359320
  87.1 0.0 copy-start.1
  87.1 1.1 %copy-done.1 = bf16[256,1536]{1,0:T(8,128)(2,1)S(1)} copy-done((bf16[256,1536]{1,0:T(8,128)(2,1)S(1)}, bf16[256,1536]{1,0:T(8,128)(2,1)}, u32[]{:S(2)}) %copy-start.1) | copy-done | bytes 786456
  88.3 0.0 copy-start.2
  88.3 1.1 %copy-done.2 = bf16[256,1536]{1,0:T(8,128)(2,1)S(1)} copy-done((bf16[256,1536]{1,0:T(8,128)(2,1)S(1)}, bf16[256,1536]{1,0:T(8,128)(2,1)}, u32[]{:S(2)}) %copy-start.2) | copy-done | bytes 786456
  89.4 0.0 copy-start.3
  89.4 1.1 %copy-done.3 = bf16[256,1536]{1,0:T(8,128)(2,1)S(1)} copy-done((bf16[256,1536]{1,0:T(8,128)(2,1)S(1)}, bf16[256,1536]{1,0:T(8,128)(2,1)}, u32[]{:S(2)}) %copy-start.3) | copy-done | bytes 786456
  90.5 3.2 %shard_map.94 = (bf16[256,1536]{1,0:T(8,128)(2,1)}, bf16[256,1536]{1,0:T(8,128)(2,1)}, bf16[256,1536]{1,0:T(8,128)(2,1)}, f32[768,1536]{1,0:T(8,128)}) custom-call(bf16[256,1536]{1,0:T(8,128)(2,1)S(1)} %copy-done.1, bf16[256,1536]{1,0:T(8,128)(2,1)S(1)} %copy-done.2, bf16[256,1536]{1,0:T(8,128)(2,1)S(1)} %copy-done.3, bf16[768,1536]{1,0:T(8,128)(2,1)S(1)} %copy-done), custom_call_target="tpu_custom_call" | custom-call | flops 1000000 | bytes 12000000 | tf_op jit(solution)/shard_map/pallas_call | solution.py:546
Async XLA Ops:
  85.5 1.7 %copy-start = (bf16[768,1536]{1,0:T(8,128)(2,1)S(1)}, bf16[768,1536]{1,0:T(8,128)(2,1)}, u32[]{:S(2)}) copy-start(bf16[768,1536]{1,0:T(8,128)(2,1)} %get-tuple-element.15.dw_ref) | copy-start | bytes 7077892
  87.1 1.1 %copy-start.1 = (bf16[256,1536]{1,0:T(8,128)(2,1)S(1)}, bf16[256,1536]{1,0:T(8,128)(2,1)}, u32[]{:S(2)}) copy-start(bf16[256,1536]{1,0:T(8,128)(2,1)} %get-tuple-element.12.dq_ref) | copy-start | bytes 2359300
  88.3 1.1 %copy-start.2 = (bf16[256,1536]{1,0:T(8,128)(2,1)S(1)}, bf16[256,1536]{1,0:T(8,128)(2,1)}, u32[]{:S(2)}) copy-start(bf16[256,1536]{1,0:T(8,128)(2,1)} %get-tuple-element.13.dk_ref) | copy-start | bytes 2359300
  89.4 1.1 %copy-start.3 = (bf16[256,1536]{1,0:T(8,128)(2,1)S(1)}, bf16[256,1536]{1,0:T(8,128)(2,1)}, u32[]{:S(2)}) copy-start(bf16[256,1536]{1,0:T(8,128)(2,1)} %get-tuple-element.14.dv_ref) | copy-start | bytes 2359300

commit v3 on v2

--- a/solution.py
+++ b/solution.py
@@ -183,12 +183,13 @@
 
 
 def fused_kernel(
-    slots, line, lists_ref, q_ref, k_ref, v_ref, og_ref, w_ref,
-    dq_ref, dk_ref, dv_ref, dw_ref,
+    slots, line, lists_ref, q_hbm, k_hbm, v_hbm, og_hbm, w_hbm,
+    dq_hbm, dk_hbm, dv_hbm, dw_hbm,
+    q_ref, k_ref, v_ref, w_ref, dq_ref, dk_ref, dv_ref, dw_ref,
     my_list, every_list, present, pick, send_k, send_v, far_k, far_v, og_halves, columns,
     columns_t, w_in, grad, attn, prob,
     own_k, own_v, back_k, back_v, came_k, came_v,
-    send_sem, recv_sem, up_send, up_recv, down_send, down_recv,
+    send_sem, recv_sem, up_send, up_recv, down_send, down_recv, load_sem, store_sem,
 ):
     rows, width = q_ref.shape
     heads = width // HD
@@ -219,6 +220,19 @@
     for move in (1, line - 1):
         pl.semaphore_signal(barrier, inc=1, device_id={"dp": (z + move) % line})
 
+    loads = []
+    for source, target in (
+        (k_hbm, k_ref),
+        (v_hbm, v_ref),
+        (og_hbm.at[:, pl.ds(0, depth)], og_halves.at[h, 0]),
+        (og_hbm.at[:, pl.ds(depth, depth)], og_halves.at[h, 1]),
+        (q_hbm, q_ref),
+        (w_hbm, w_ref),
+    ):
+        loads.append(pltpu.make_async_copy(source, target, load_sem.at[len(loads)]))
+        loads[-1].start()
+    load_k, load_v, load_og0, load_og1, load_q, load_w = loads
+
     for entry in range(entries):
         named = lists_ref[entry // RET, entry % RET]
         my_list[entry : entry + 1, :] = jnp.full((1, rows), named, jnp.int32)
@@ -254,16 +268,11 @@
     for chunk in range(chunks):
         crossing.append(
             send(
-                w_ref.at[piece_rows(z), chunk_cols(chunk)],
+                w_hbm.at[piece_rows(z), chunk_cols(chunk)],
                 w_in.at[PARTNER, chunk, piece_rows(z)],
                 to(PARTNER),
             )
         )
-    mate_w = [
-        send(w_ref.at[:, chunk_cols(chunk)], w_in.at[MATE, chunk], to(MATE))
-        for chunk in range(chunks)
-    ]
-
     def hop(chunk, step, upward):
         move = 1 if upward else -1
         index = z - step if upward else z + step
@@ -305,10 +314,10 @@
 
     halves_in = []
     for part in range(2):
-        og_halves[h, part] = og_ref[:, part * depth : (part + 1) * depth]
-    for part in range(2):
         halves_in.append(
-            send(og_halves.at[h, part], og_halves.at[h, part], {"head": 1 - h})
+            send(
+                og_hbm.at[:, pl.ds(part * depth, depth)], og_halves.at[h, part], {"head": 1 - h}
+            )
         )
     for copy in lists_in:
         copy.wait_recv()
@@ -358,9 +367,11 @@
         send_v[:, cols] = dot(pick[...], v_ref[:, cols]).astype(BF16)
 
     frames_in = []
+    load_k.wait()
     tiled(pick_keys)
     for kind in (PARTNER, DIAG, MATE):
         frames_in.append(send(send_k.at[span_of(kind)], far_k.at[span_of(kind)], to(kind)))
+    load_v.wait()
     tiled(pick_values)
     for kind in (PARTNER, DIAG, MATE):
         frames_in.append(send(send_v.at[span_of(kind)], far_v.at[span_of(kind)], to(kind)))
@@ -370,6 +381,8 @@
 
     hop_start(0, 0)
     hop_start(0, 1)
+    load_og0.wait()
+    load_og1.wait()
     for copy in halves_in:
         copy.wait_recv()
     mine = pl.ds(pl.multiple_of(h * half_rows, half_rows), half_rows)
@@ -383,8 +396,13 @@
     columns[SELF] = og_halves[t // 2, t % 2]
     hop_start(0, 2)
     hop_start(1, 0)
+    mate_w = [
+        send(w_hbm.at[:, chunk_cols(chunk)], w_in.at[MATE, chunk], to(MATE))
+        for chunk in range(chunks)
+    ]
     hop_start(1, 1)
 
+    load_q.wait()
     for copy in frames_in:
         copy.wait_recv()
 
@@ -460,6 +478,13 @@
         back_v[:, cols] = far_dv.astype(BF16)
         return carry
 
+    stores = []
+
+    def store(source, target):
+        stores.append(pltpu.make_async_copy(source, target, store_sem.at[len(stores)]))
+        stores[-1].start()
+
+    load_w.wait()
     returned = []
     step_width = 384
     for chunk in range(chunks):
@@ -489,6 +514,7 @@
                 returned.append(
                     send(out.at[span_of(kind), cols], into.at[span_of(kind), cols], to(kind))
                 )
+        store(dq_ref.at[:, cols], dq_hbm.at[:, cols])
     came_k[0:far_rows, :] = back_k[0:far_rows, :]
     came_v[0:far_rows, :] = back_v[0:far_rows, :]
     attn_diag = []
@@ -511,14 +537,23 @@
         dw_ref[:, cols] = total.astype(BF16)
 
     tiled(weight_part)
-    for copy in returned:
-        copy.wait_recv()
-
-    def add_returned(cols):
+    store(dw_ref, dw_hbm)
+
+    def add_returned(i, carry):
+        cols = pl.ds(pl.multiple_of(i * step_width, step_width), step_width)
         dk_ref[:, cols] = (own_k[:, cols] + dotx(pick[...], came_k[:, cols], TN)).astype(BF16)
         dv_ref[:, cols] = (own_v[:, cols] + dotx(pick[...], came_v[:, cols], TN)).astype(BF16)
-
-    tiled(add_returned)
+        return carry
+
+    per_chunk = len(returned) // chunks
+    for chunk in range(chunks):
+        for copy in returned[chunk * per_chunk : (chunk + 1) * per_chunk]:
+            copy.wait_recv()
+        steps = span_width // step_width
+        lax.fori_loop(chunk * steps, (chunk + 1) * steps, add_returned, 0)
+        cols = chunk_cols(chunk)
+        store(dk_ref.at[:, cols], dk_hbm.at[:, cols])
+        store(dv_ref.at[:, cols], dv_hbm.at[:, cols])
     for copy in started:
         copy.wait_send()
     for chunk in range(chunks):
@@ -528,6 +563,9 @@
                 @pl.when(hop_sent(step, upward))
                 def left():
                     hop(chunk, step, upward).wait_send()
+
+    for copy in stores:
+        copy.wait()
 
 
 def finish_kernel(dq_ref, dk_ref, dv_ref, dw_ref, dq_out, dk_out, dv_out, dw_out):
@@ -550,7 +588,7 @@
         + [jax.ShapeDtypeStruct((depth, width), F32)],
         in_specs=[small, small, small, large],
         out_specs=[small, small, small, large],
-        compiler_params=pltpu.CompilerParams(vmem_limit_bytes=32 * 1024 * 1024),
+        compiler_params=pltpu.CompilerParams(vmem_limit_bytes=60 * 1024 * 1024),
         cost_estimate=pl.CostEstimate(flops=10**6, bytes_accessed=12 * 10**6, transcendentals=0),
     )(dq, dk, dv, dw)
 
@@ -563,7 +601,7 @@
     heads = width // HD
     flat = [x.reshape(rows, width) for x in (queries, keys, values, out_grad)]
     line = lax.axis_size("dp")
-    vmem = pl.BlockSpec(memory_space=pltpu.VMEM)
+    hbm = pl.BlockSpec(memory_space=pl.ANY)
     far = 4 * slots * frame_tokens
 
     def low(*shape):
@@ -576,9 +614,17 @@
         functools.partial(fused_kernel, slots, line),
         out_shape=[jax.ShapeDtypeStruct((rows, width), BF16)] * 3
         + [jax.ShapeDtypeStruct((depth, width), BF16)],
-        in_specs=[pl.BlockSpec(memory_space=pltpu.SMEM)] + [vmem] * 5,
-        out_specs=[vmem] * 4,
+        in_specs=[pl.BlockSpec(memory_space=pltpu.SMEM)] + [hbm] * 5,
+        out_specs=[hbm] * 4,
         scratch_shapes=[
+            low(rows, width),
+            low(rows, width),
+            low(rows, width),
+            low(depth, width),
+            low(rows, width),
+            low(rows, width),
+            low(rows, width),
+            low(depth, width),
             pltpu.VMEM((lists.size, rows), jnp.int32),
             pltpu.VMEM((4, lists.size, rows), jnp.int32),
             low(4 * frame_tokens, rows),
@@ -606,6 +652,8 @@
             pltpu.SemaphoreType.DMA((2, line - 1)),
             pltpu.SemaphoreType.DMA((2, line - 1)),
             pltpu.SemaphoreType.DMA((2, line - 1)),
+            pltpu.SemaphoreType.DMA((6,)),
+            pltpu.SemaphoreType.DMA((7,)),
         ],
         compiler_params=pltpu.CompilerParams(
             collective_id=0, has_side_effects=True, vmem_limit_bytes=60 * 1024 * 1024

time: 95.5 us -> 89.4 us (0.936)
  local copies, waits for them, and re-layouts: 5.06 us -> 0 us
  Pallas kernels: 88 us -> 87 us
    unnamed x8 -> x0, local copies, waits for them, and re-layouts: 5.06 us -> none
    pallas_call x1, Pallas kernels: 84.8 us -> 81.3 us  [fused(): pl.pallas_call(functools.partial(fused_kernel, slots, line), out_shape=[j...]
    pallas_call x1, Pallas kernels: 3.15 us -> 5.69 us  [finish(): pl.pallas_call(finish_kernel, grid=(steps,), out_shape=[jax.ShapeDtypeStr...]
where the time goes in v3:
time: 89.4 us; the launch traced here: 87.7 us
  Pallas kernels  87 us (97%)
    pallas_call x1, Pallas kernels, fused(): pl.pallas_call(functools.partial(fused_kernel, slots, line), out_shape=[j...  81.3 us
    pallas_call x1, Pallas kernels, finish(): pl.pallas_call(finish_kernel, grid=(steps,), out_shape=[jax.ShapeDtypeStr...  5.69 us

profile of v3, /device:TPU:1, one launch (start us, length us, event | category | flops | bytes accessed | tf_op | source)
XLA Modules:
  0.0 87.7 jit_solution(605037619431241728)
XLA Ops:
  0.6 81.3 %shard_map.93 = (bf16[256,1536]{1,0:T(8,128)(2,1)}, bf16[256,1536]{1,0:T(8,128)(2,1)}, bf16[256,1536]{1,0:T(8,128)(2,1)}, bf16[768,1536]{1,0:T(8,128)(2,1)}) custom-call(s32[2,8]{1,0:T(2,128)} %lists_ref.1, bf16[256,1536]{1,0:T(8,128)(2,1)} %bitcast.7, bf16[256,1536]{1,0:T(8,128)(2,1)} %bitcast.8, bf16[256,1536]{1,0:T(8,128)(2,1)} %bitcast.9, ...), custom_call_target="tpu_custom_call" | custom-call | flops 7000000000 | bytes 16000000 | tf_op jit(solution)/shard_map/pallas_call | solution.py:613
  82.0 5.7 %shard_map.94 = (bf16[256,1536]{1,0:T(8,128)(2,1)}, bf16[256,1536]{1,0:T(8,128)(2,1)}, bf16[256,1536]{1,0:T(8,128)(2,1)}, f32[768,1536]{1,0:T(8,128)}) custom-call(bf16[256,1536]{1,0:T(8,128)(2,1)} %get-tuple-element.12.dq_ref, bf16[256,1536]{1,0:T(8,128)(2,1)} %get-tuple-element.13.dk_ref, bf16[256,1536]{1,0:T(8,128)(2,1)} %get-tuple-element.14.dv_ref, ...), custom_call_target="tpu_custom_call" | custom-call | flops 1000000 | bytes 12000000 | tf_op jit(solution)/shard_map/pallas_call | solution.py:584

commit v4 on v3

--- a/solution.py
+++ b/solution.py
@@ -184,12 +184,13 @@
 
 def fused_kernel(
     slots, line, lists_ref, q_hbm, k_hbm, v_hbm, og_hbm, w_hbm,
-    dq_hbm, dk_hbm, dv_hbm, dw_hbm,
-    q_ref, k_ref, v_ref, w_ref, dq_ref, dk_ref, dv_ref, dw_ref,
+    dq_ref, dk_ref, dv_ref, dw_ref,
+    q_ref, k_ref, v_ref, w_ref,
     my_list, every_list, present, pick, send_k, send_v, far_k, far_v, og_halves, columns,
     columns_t, w_in, grad, attn, prob,
     own_k, own_v, back_k, back_v, came_k, came_v,
-    send_sem, recv_sem, up_send, up_recv, down_send, down_recv, load_sem, store_sem,
+    send_sem, recv_sem, up_send, up_recv, down_send, down_recv, load_sem,
+    relay_send, relay_recv,
 ):
     rows, width = q_ref.shape
     heads = width // HD
@@ -294,12 +295,36 @@
             return z - 1 - step >= 0
         return z + 1 + step < line
 
+    def relay(chunk, step, upward):
+        index = jnp.clip(z - 1 - step if upward else z + 1 + step, 0, line - 1)
+        place = 2 * step + (0 if upward else 1)
+        return pltpu.make_async_remote_copy(
+            src_ref=w_in.at[PARTNER, chunk, piece_rows(index)],
+            dst_ref=w_in.at[DIAG, chunk, piece_rows(index)],
+            send_sem=relay_send.at[chunk, place], recv_sem=relay_recv.at[chunk, place],
+            device_id=to(MATE),
+        )
+
+    def relay_done(chunk, received):
+        for step in range(line - 1):
+            for upward in (True, False):
+
+                @pl.when(hop_received(step, upward))
+                def done():
+                    if received:
+                        relay(chunk, step, upward).wait_recv()
+                    else:
+                        relay(chunk, step, upward).wait_send()
+
     def hop_wait(chunk, step):
         for upward in (True, False):
 
             @pl.when(hop_received(step, upward))
             def arrived():
                 hop(chunk, step, upward).wait_recv()
+                relay(chunk, step, upward).start()
+
+    diag_w = []
 
     def hop_start(chunk, step):
         if step == 0:
@@ -311,6 +336,15 @@
             @pl.when(hop_sent(step, upward))
             def onward():
                 hop(chunk, step, upward).start()
+
+        if step == 0:
+            diag_w.append(
+                send(
+                    w_in.at[PARTNER, chunk, piece_rows(z)],
+                    w_in.at[DIAG, chunk, piece_rows(z)],
+                    to(MATE),
+                )
+            )
 
     halves_in = []
     for part in range(2):
@@ -440,7 +474,6 @@
         if chunk == 0:
             hop_start(1, 2)
             hop_wait(0, 2)
-            diag_w = [send(w_in.at[PARTNER, 0], w_in.at[DIAG, 0], to(MATE))]
     swapped = []
     for kind in (PARTNER, DIAG):
         columns_in[kind].wait_recv()
@@ -478,43 +511,30 @@
         back_v[:, cols] = far_dv.astype(BF16)
         return carry
 
-    stores = []
-
-    def store(source, target):
-        stores.append(pltpu.make_async_copy(source, target, store_sem.at[len(stores)]))
-        stores[-1].start()
-
     load_w.wait()
     returned = []
-    step_width = 384
-    for chunk in range(chunks):
-        if chunk == 1:
-            hop_wait(1, 2)
-            diag_w.append(send(w_in.at[PARTNER, 1], w_in.at[DIAG, 1], to(MATE)))
-        mate_w[chunk].wait_recv()
-        diag_w[chunk].wait_recv()
-
-        def project(i, carry):
-            local = pl.ds(pl.multiple_of(i * step_width, step_width), step_width)
-            there = pl.ds(
-                pl.multiple_of(chunk * span_width + i * step_width, step_width), step_width
-            )
-            total = dot(og_halves[t // 2, t % 2], w_ref[:, there])
-            for kind in (MATE, PARTNER, DIAG):
-                peer = peers[kind]
-                total += dot(og_halves[peer // 2, peer % 2], w_in[kind, chunk, :, local])
-            grad[:, there] = total.astype(BF16)
-            return carry
-
-        lax.fori_loop(0, span_width // step_width, project, 0)
-        lax.fori_loop(chunk * each, (chunk + 1) * each, backward, 0)
-        cols = chunk_cols(chunk)
+    step_width = span_width // 2
+    for part in range(2 * chunks):
+        chunk = part // 2
+        if part % 2 == 0:
+            if chunk == 1:
+                hop_wait(1, 2)
+            mate_w[chunk].wait_recv()
+            diag_w[chunk].wait_recv()
+            relay_done(chunk, True)
+        local = pl.ds(part % 2 * step_width, step_width)
+        cols = pl.ds(part * step_width, step_width)
+        total = dot(og_halves[t // 2, t % 2], w_ref[:, cols])
+        for kind in (MATE, PARTNER, DIAG):
+            peer = peers[kind]
+            total += dot(og_halves[peer // 2, peer % 2], w_in[kind, chunk, :, local])
+        grad[:, cols] = total.astype(BF16)
+        lax.fori_loop(part * each // 2, (part + 1) * each // 2, backward, 0)
         for kind in (PARTNER, DIAG, MATE):
             for out, into in ((back_k, came_k), (back_v, came_v)):
                 returned.append(
                     send(out.at[span_of(kind), cols], into.at[span_of(kind), cols], to(kind))
                 )
-        store(dq_ref.at[:, cols], dq_hbm.at[:, cols])
     came_k[0:far_rows, :] = back_k[0:far_rows, :]
     came_v[0:far_rows, :] = back_v[0:far_rows, :]
     attn_diag = []
@@ -534,26 +554,17 @@
         total = dot(columns_t[SELF], attn[SELF, :, cols])
         for kind in (MATE, PARTNER, DIAG):
             total += dot(columns_t[kind], attn[kind, :, cols])
-        dw_ref[:, cols] = total.astype(BF16)
+        dw_ref[:, cols] = total
 
     tiled(weight_part)
-    store(dw_ref, dw_hbm)
-
-    def add_returned(i, carry):
-        cols = pl.ds(pl.multiple_of(i * step_width, step_width), step_width)
+
+    per_part = len(returned) // (2 * chunks)
+    for part in range(2 * chunks):
+        for copy in returned[part * per_part : (part + 1) * per_part]:
+            copy.wait_recv()
+        cols = pl.ds(part * step_width, step_width)
         dk_ref[:, cols] = (own_k[:, cols] + dotx(pick[...], came_k[:, cols], TN)).astype(BF16)
         dv_ref[:, cols] = (own_v[:, cols] + dotx(pick[...], came_v[:, cols], TN)).astype(BF16)
-        return carry
-
-    per_chunk = len(returned) // chunks
-    for chunk in range(chunks):
-        for copy in returned[chunk * per_chunk : (chunk + 1) * per_chunk]:
-            copy.wait_recv()
-        steps = span_width // step_width
-        lax.fori_loop(chunk * steps, (chunk + 1) * steps, add_returned, 0)
-        cols = chunk_cols(chunk)
-        store(dk_ref.at[:, cols], dk_hbm.at[:, cols])
-        store(dv_ref.at[:, cols], dv_hbm.at[:, cols])
     for copy in started:
         copy.wait_send()
     for chunk in range(chunks):
@@ -564,32 +575,37 @@
                 def left():
                     hop(chunk, step, upward).wait_send()
 
-    for copy in stores:
+    for chunk in range(chunks):
+        relay_done(chunk, False)
+
+
+def finish_kernel(dq_ref, dk_ref, dv_ref, dw_ref, dq_out, dk_out, dv_out, dw_out, sem):
+    copies = [
+        pltpu.make_async_copy(source, target, sem.at[number])
+        for number, (source, target) in enumerate(
+            ((dw_ref, dw_out), (dq_ref, dq_out), (dk_ref, dk_out), (dv_ref, dv_out))
+        )
+    ]
+    for copy in copies:
+        copy.start()
+    for copy in copies:
         copy.wait()
 
 
-def finish_kernel(dq_ref, dk_ref, dv_ref, dw_ref, dq_out, dk_out, dv_out, dw_out):
-    dq_out[...] = dq_ref[...]
-    dk_out[...] = dk_ref[...]
-    dv_out[...] = dv_ref[...]
-    dw_out[...] = dw_ref[...].astype(F32)
-
-
 def finish(dq, dk, dv, dw):
-    steps = 4
     rows, width = dq.shape
     depth = dw.shape[0]
-    small = pl.BlockSpec((rows // steps, width), lambda i: (i, 0))
-    large = pl.BlockSpec((depth // steps, width), lambda i: (i, 0))
+    vmem = pl.BlockSpec(memory_space=pltpu.VMEM)
+    hbm = pl.BlockSpec(memory_space=pltpu.HBM)
     return pl.pallas_call(
         finish_kernel,
-        grid=(steps,),
         out_shape=[jax.ShapeDtypeStruct((rows, width), BF16)] * 3
         + [jax.ShapeDtypeStruct((depth, width), F32)],
-        in_specs=[small, small, small, large],
-        out_specs=[small, small, small, large],
-        compiler_params=pltpu.CompilerParams(vmem_limit_bytes=60 * 1024 * 1024),
-        cost_estimate=pl.CostEstimate(flops=10**6, bytes_accessed=12 * 10**6, transcendentals=0),
+        in_specs=[vmem] * 4,
+        out_specs=[hbm] * 4,
+        scratch_shapes=[pltpu.SemaphoreType.DMA((4,))],
+        compiler_params=pltpu.CompilerParams(vmem_limit_bytes=16 * 1024 * 1024),
+        cost_estimate=pl.CostEstimate(flops=0, bytes_accessed=7 * 10**6, transcendentals=0),
     )(dq, dk, dv, dw)
 
 
@@ -601,7 +617,7 @@
     heads = width // HD
     flat = [x.reshape(rows, width) for x in (queries, keys, values, out_grad)]
     line = lax.axis_size("dp")
-    hbm = pl.BlockSpec(memory_space=pl.ANY)
+    hbm = pl.BlockSpec(memory_space=pltpu.HBM)
     far = 4 * slots * frame_tokens
 
     def low(*shape):
@@ -612,15 +628,10 @@
 
     dq, dk, dv, dw = pl.pallas_call(
         functools.partial(fused_kernel, slots, line),
-        out_shape=[jax.ShapeDtypeStruct((rows, width), BF16)] * 3
-        + [jax.ShapeDtypeStruct((depth, width), BF16)],
+        out_shape=[pltpu.VMEM((rows, width), BF16)] * 3 + [pltpu.VMEM((depth, width), F32)],
         in_specs=[pl.BlockSpec(memory_space=pltpu.SMEM)] + [hbm] * 5,
-        out_specs=[hbm] * 4,
+        out_specs=[pl.BlockSpec(memory_space=pltpu.VMEM)] * 4,
         scratch_shapes=[
-            low(rows, width),
-            low(rows, width),
-            low(rows, width),
-            low(depth, width),
             low(rows, width),
             low(rows, width),
             low(rows, width),
@@ -646,17 +657,18 @@
             low(far, width),
             low(far, width),
             low(far, width),
-            pltpu.SemaphoreType.DMA((48,)),
-            pltpu.SemaphoreType.DMA((48,)),
+            pltpu.SemaphoreType.DMA((64,)),
+            pltpu.SemaphoreType.DMA((64,)),
             pltpu.SemaphoreType.DMA((2, line - 1)),
             pltpu.SemaphoreType.DMA((2, line - 1)),
             pltpu.SemaphoreType.DMA((2, line - 1)),
             pltpu.SemaphoreType.DMA((2, line - 1)),
             pltpu.SemaphoreType.DMA((6,)),
-            pltpu.SemaphoreType.DMA((7,)),
+            pltpu.SemaphoreType.DMA((2, 2 * (line - 1))),
+            pltpu.SemaphoreType.DMA((2, 2 * (line - 1))),
         ],
         compiler_params=pltpu.CompilerParams(
-            collective_id=0, has_side_effects=True, vmem_limit_bytes=60 * 1024 * 1024
+            collective_id=0, has_side_effects=True, vmem_limit_bytes=50 * 1024 * 1024
         ),
         cost_estimate=pl.CostEstimate(
             flops=7 * 10**9, bytes_accessed=16 * 10**6, transcendentals=10**6

time: 89.4 us -> 85.3 us (0.954); the launches traced: 87.7 us -> 85.2 us
  Pallas kernels: 87 us -> 84.5 us
    pallas_call x2, Pallas kernels: 87 us -> 84.5 us  [the longest x1 81.6 us: fused(): pl.pallas_call(functools.partial(fused_kernel, slots, line), out_shape=[p...]
where the time goes in v4:
time: 85.3 us; the launch traced here: 85.2 us
  Pallas kernels  84.5 us (99%)
    pallas_call x1, Pallas kernels, fused(): pl.pallas_call(functools.partial(fused_kernel, slots, line), out_shape=[p...  81.6 us
    pallas_call x1, Pallas kernels, finish(): pl.pallas_call(finish_kernel, out_shape=[jax.ShapeDtypeStruct((rows, widt...  2.94 us

profile of v4, /device:TPU:1, one launch (start us, length us, event | category | flops | bytes accessed | tf_op | source)
XLA Modules:
  0.0 85.2 jit_solution(11837199157956663194)
XLA Ops:
  0.6 81.6 %shard_map.93 = (bf16[256,1536]{1,0:T(8,128)(2,1)S(1)}, bf16[256,1536]{1,0:T(8,128)(2,1)S(1)}, bf16[256,1536]{1,0:T(8,128)(2,1)S(1)}, f32[768,1536]{1,0:T(8,128)S(1)}) custom-call(s32[2,8]{1,0:T(2,128)} %lists_ref.1, bf16[256,1536]{1,0:T(8,128)(2,1)} %bitcast.7, bf16[256,1536]{1,0:T(8,128)(2,1)} %bitcast.8, bf16[256,1536]{1,0:T(8,128)(2,1)} %bitcast.9, ...), custom_call_target="tpu_custom_call" | custom-call | flops 7000000000 | bytes 16000000 | tf_op jit(solution)/shard_map/pallas_call | solution.py:629
  82.2 2.9 %shard_map.94 = (bf16[256,1536]{1,0:T(8,128)(2,1)}, bf16[256,1536]{1,0:T(8,128)(2,1)}, bf16[256,1536]{1,0:T(8,128)(2,1)}, f32[768,1536]{1,0:T(8,128)}) custom-call(bf16[256,1536]{1,0:T(8,128)(2,1)S(1)} %get-tuple-element.12.dq_ref, bf16[256,1536]{1,0:T(8,128)(2,1)S(1)} %get-tuple-element.13.dk_ref, bf16[256,1536]{1,0:T(8,128)(2,1)S(1)} %get-tuple-element.14.dv_ref, ...), custom_call_target="tpu_custom_call" | custom-call | bytes 7000000 | tf_op jit(solution)/shard_map/pallas_call | solution.py:600

commit v5 on v4

--- a/solution.py
+++ b/solution.py
@@ -194,7 +194,7 @@
 ):
     rows, width = q_ref.shape
     heads = width // HD
-    entries = my_list.shape[0]
+    entries, lanes = my_list.shape
     frame_tokens = 32
     group_rows = CF * frame_tokens
     groups = rows // group_rows
@@ -218,8 +218,13 @@
         pl.semaphore_signal(barrier, inc=1, device_id={"tm": peers[kind]})
     pl.semaphore_signal(barrier, inc=1, device_id={"head": 1 - h})
 
-    for move in (1, line - 1):
-        pl.semaphore_signal(barrier, inc=1, device_id={"dp": (z + move) % line})
+    @pl.when(z > 0)
+    def greet_below():
+        pl.semaphore_signal(barrier, inc=1, device_id={"dp": z - 1})
+
+    @pl.when(z < line - 1)
+    def greet_above():
+        pl.semaphore_signal(barrier, inc=1, device_id={"dp": z + 1})
 
     loads = []
     for source, target in (
@@ -236,9 +241,10 @@
 
     for entry in range(entries):
         named = lists_ref[entry // RET, entry % RET]
-        my_list[entry : entry + 1, :] = jnp.full((1, rows), named, jnp.int32)
-        every_list[SELF, entry : entry + 1, :] = jnp.full((1, rows), named, jnp.int32)
-    pl.semaphore_wait(barrier, 6)
+        my_list[entry : entry + 1, :] = jnp.full((1, lanes), named, jnp.int32)
+        every_list[SELF, entry : entry + 1, :] = jnp.full((1, lanes), named, jnp.int32)
+    sides = (z + line - 1) // line + (2 * line - 2 - z) // line
+    pl.semaphore_wait(barrier, 4 + sides)
 
     started = []
 
@@ -356,13 +362,17 @@
     for copy in lists_in:
         copy.wait_recv()
 
-    lanes = lax.broadcasted_iota(jnp.int32, (entries, rows), 1)
-    my_frame = t * (rows // frame_tokens) + lax.shift_right_logical(lanes, 5)
-    for kind in range(4):
-        named = jnp.max((every_list[kind] == my_frame).astype(F32), axis=0, keepdims=True)
-        present[kind * frame_tokens : (kind + 1) * frame_tokens, :] = jnp.broadcast_to(
-            named, (frame_tokens, rows)
-        ).astype(BF16)
+    lane_frame = lax.shift_right_logical(
+        lax.broadcasted_iota(jnp.int32, (entries, lanes), 1), 5
+    )
+    for side in range(rows // lanes):
+        my_frame = (t * rows + side * lanes) // frame_tokens + lane_frame
+        for kind in range(4):
+            named = jnp.max((every_list[kind] == my_frame).astype(F32), axis=0, keepdims=True)
+            present[
+                kind * frame_tokens : (kind + 1) * frame_tokens,
+                side * lanes : (side + 1) * lanes,
+            ] = jnp.broadcast_to(named, (frame_tokens, lanes)).astype(BF16)
     above = lax.broadcasted_iota(jnp.int32, (rows, rows), 0)
     below = lax.broadcasted_iota(jnp.int32, (rows, rows), 1)
     earlier = (
@@ -580,11 +590,16 @@
 
 
 def finish_kernel(dq_ref, dk_ref, dv_ref, dw_ref, dq_out, dk_out, dv_out, dw_out, sem):
+    parts = 4
+    piece = dw_ref.shape[0] // parts
+    pairs = [
+        (dw_ref.at[pl.ds(i * piece, piece)], dw_out.at[pl.ds(i * piece, piece)])
+        for i in range(parts)
+    ]
+    pairs += [(dq_ref, dq_out), (dk_ref, dk_out), (dv_ref, dv_out)]
     copies = [
         pltpu.make_async_copy(source, target, sem.at[number])
-        for number, (source, target) in enumerate(
-            ((dw_ref, dw_out), (dq_ref, dq_out), (dk_ref, dk_out), (dv_ref, dv_out))
-        )
+        for number, (source, target) in enumerate(pairs)
     ]
     for copy in copies:
         copy.start()
@@ -603,7 +618,7 @@
         + [jax.ShapeDtypeStruct((depth, width), F32)],
         in_specs=[vmem] * 4,
         out_specs=[hbm] * 4,
-        scratch_shapes=[pltpu.SemaphoreType.DMA((4,))],
+        scratch_shapes=[pltpu.SemaphoreType.DMA((7,))],
         compiler_params=pltpu.CompilerParams(vmem_limit_bytes=16 * 1024 * 1024),
         cost_estimate=pl.CostEstimate(flops=0, bytes_accessed=7 * 10**6, transcendentals=0),
     )(dq, dk, dv, dw)
@@ -636,8 +651,8 @@
             low(rows, width),
             low(rows, width),
             low(depth, width),
-            pltpu.VMEM((lists.size, rows), jnp.int32),
-            pltpu.VMEM((4, lists.size, rows), jnp.int32),
+            pltpu.VMEM((lists.size, 128), jnp.int32),
+            pltpu.VMEM((4, lists.size, 128), jnp.int32),
             low(4 * frame_tokens, rows),
             low(far, rows),
             low(far, width),

time: 85.3 us -> 85.1 us (level)
  no operation moved by 1% of the time
where the time goes in v5:
time: 85.1 us; the launch traced here: 85 us
  Pallas kernels  84.3 us (99%)
    pallas_call x1, Pallas kernels, fused(): pl.pallas_call(functools.partial(fused_kernel, slots, line), out_shape=[p...  81.4 us
    pallas_call x1, Pallas kernels, finish(): pl.pallas_call(finish_kernel, out_shape=[jax.ShapeDtypeStruct((rows, widt...  2.97 us

profile of v5, /device:TPU:1, one launch (start us, length us, event | category | flops | bytes accessed | tf_op | source)
XLA Modules:
  0.0 85.0 jit_solution(766683783713188550)
XLA Ops:
  0.6 81.4 %shard_map.93 = (bf16[256,1536]{1,0:T(8,128)(2,1)S(1)}, bf16[256,1536]{1,0:T(8,128)(2,1)S(1)}, bf16[256,1536]{1,0:T(8,128)(2,1)S(1)}, f32[768,1536]{1,0:T(8,128)S(1)}) custom-call(s32[2,8]{1,0:T(2,128)} %lists_ref.1, bf16[256,1536]{1,0:T(8,128)(2,1)} %bitcast.7, bf16[256,1536]{1,0:T(8,128)(2,1)} %bitcast.8, bf16[256,1536]{1,0:T(8,128)(2,1)} %bitcast.9, ...), custom_call_target="tpu_custom_call" | custom-call | flops 7000000000 | bytes 16000000 | tf_op jit(solution)/shard_map/pallas_call | solution.py:644
  82.0 3.0 %shard_map.94 = (bf16[256,1536]{1,0:T(8,128)(2,1)}, bf16[256,1536]{1,0:T(8,128)(2,1)}, bf16[256,1536]{1,0:T(8,128)(2,1)}, f32[768,1536]{1,0:T(8,128)}) custom-call(bf16[256,1536]{1,0:T(8,128)(2,1)S(1)} %get-tuple-element.12.dq_ref, bf16[256,1536]{1,0:T(8,128)(2,1)S(1)} %get-tuple-element.13.dk_ref, bf16[256,1536]{1,0:T(8,128)(2,1)S(1)} %get-tuple-element.14.dv_ref, ...), custom_call_target="tpu_custom_call" | custom-call | bytes 7000000 | tf_op jit(solution)/shard_map/pallas_call | solution.py:615

commit v6 on v5

--- a/solution.py
+++ b/solution.py
@@ -450,34 +450,45 @@
     for copy in frames_in:
         copy.wait_recv()
 
-    def forward(i, carry):
+    spans = [slice(g * group_rows, (g + 1) * group_rows) for g in range(groups)]
+
+    def by_group(product):
+        return jnp.concatenate([product(span) for span in spans], axis=0)
+
+    def forward_head(i):
         cols = pl.ds(pl.multiple_of(i * HD, HD), HD)
-        fk = far_k[:, cols]
-        fv = far_v[:, cols]
-        for g in range(groups):
-            span = slice(g * group_rows, (g + 1) * group_rows)
-            q = q_ref[span, cols]
-            near = dotx(q, k_ref[span, cols], NT) * scale
-            far = dotx(q, fk, NT) * scale
-            top = jnp.maximum(
-                jnp.max(near, axis=1, keepdims=True), jnp.max(far, axis=1, keepdims=True)
-            )
-            near = jnp.exp(near - top)
-            far = jnp.exp(far - top)
-            total = jnp.sum(near, axis=1, keepdims=True) + jnp.sum(far, axis=1, keepdims=True)
-            near = near / total
-            far = far / total
-            prob[i, span, 0:group_rows] = near
-            prob[i, span, group_rows:] = far
-            out = dot(near.astype(BF16), v_ref[span, cols]) + dot(far.astype(BF16), fv)
-            attn[SELF, span, cols] = out.astype(BF16)
-        return carry
-
+        near = by_group(lambda span: dotx(q_ref[span, cols], k_ref[span, cols], NT)) * scale
+        far = dotx(q_ref[:, cols], far_k[:, cols], NT) * scale
+        top = jnp.maximum(
+            jnp.max(near, axis=1, keepdims=True), jnp.max(far, axis=1, keepdims=True)
+        )
+        near = jnp.exp(near - top)
+        far = jnp.exp(far - top)
+        total = jnp.sum(near, axis=1, keepdims=True) + jnp.sum(far, axis=1, keepdims=True)
+        near = near / total
+        far = far / total
+        prob[i, :, 0:group_rows] = near
+        prob[i, :, group_rows:] = far
+        near_low = near.astype(BF16)
+        out = by_group(lambda span: dot(near_low[span], v_ref[span, cols]))
+        attn[SELF, :, cols] = (out + dot(far.astype(BF16), far_v[:, cols])).astype(BF16)
+
+    together = 3
+
+    def several(head):
+        def body(i, carry):
+            for place in range(together):
+                head(i * together + place)
+            return carry
+
+        return body
+
+    forward = several(forward_head)
     each = heads // chunks
     attn_partner = []
     attn_mate = []
     for chunk in range(chunks):
-        lax.fori_loop(chunk * each, (chunk + 1) * each, forward, 0)
+        lax.fori_loop(chunk * each // together, (chunk + 1) * each // together, forward, 0)
         own = attn.at[SELF, :, chunk_cols(chunk)]
         attn_mate.append(send(own, attn.at[MATE, :, chunk_cols(chunk)], to(MATE)))
         attn_partner.append(send(own, attn.at[PARTNER, :, chunk_cols(chunk)], to(PARTNER)))
@@ -489,38 +500,27 @@
         columns_in[kind].wait_recv()
         swapped.append(send(columns.at[kind, mine], columns.at[kind, mine], {"head": 1 - h}))
 
-    def backward(i, carry):
+    def backward_head(i):
         cols = pl.ds(pl.multiple_of(i * HD, HD), HD)
-        fk = far_k[:, cols]
-        fv = far_v[:, cols]
-        far_dk = None
-        far_dv = None
-        for g in range(groups):
-            span = slice(g * group_rows, (g + 1) * group_rows)
-            q = q_ref[span, cols]
-            do = grad[span, cols]
-            row_dot = jnp.sum(
-                do.astype(F32) * attn[SELF, span, cols].astype(F32), axis=1, keepdims=True
-            )
-            near = prob[i, span, 0:group_rows]
-            far = prob[i, span, group_rows:]
-            near_ds = (near * (dotx(do, v_ref[span, cols], NT) - row_dot)).astype(BF16)
-            far_ds = (far * (dotx(do, fv, NT) - row_dot)).astype(BF16)
-            near_p = near.astype(BF16)
-            far_p = far.astype(BF16)
-            dq_ref[span, cols] = (
-                (dot(near_ds, k_ref[span, cols]) + dot(far_ds, fk)) * scale
-            ).astype(BF16)
-            own_k[span, cols] = dotx(near_ds, q, TN) * scale
-            own_v[span, cols] = dotx(near_p, do, TN)
-            more_k = dotx(far_ds, q, TN)
-            more_v = dotx(far_p, do, TN)
-            far_dk = more_k if g == 0 else far_dk + more_k
-            far_dv = more_v if g == 0 else far_dv + more_v
-        back_k[:, cols] = (far_dk * scale).astype(BF16)
-        back_v[:, cols] = far_dv.astype(BF16)
-        return carry
-
+        q = q_ref[:, cols]
+        do = grad[:, cols]
+        row_dot = jnp.sum(
+            do.astype(F32) * attn[SELF, :, cols].astype(F32), axis=1, keepdims=True
+        )
+        near = prob[i, :, 0:group_rows]
+        far = prob[i, :, group_rows:]
+        near_dp = by_group(lambda span: dotx(do[span], v_ref[span, cols], NT))
+        near_ds = (near * (near_dp - row_dot)).astype(BF16)
+        far_ds = (far * (dotx(do, far_v[:, cols], NT) - row_dot)).astype(BF16)
+        near_p = near.astype(BF16)
+        near_dq = by_group(lambda span: dot(near_ds[span], k_ref[span, cols]))
+        dq_ref[:, cols] = ((near_dq + dot(far_ds, far_k[:, cols])) * scale).astype(BF16)
+        own_k[:, cols] = by_group(lambda span: dotx(near_ds[span], q[span], TN)) * scale
+        own_v[:, cols] = by_group(lambda span: dotx(near_p[span], do[span], TN))
+        back_k[:, cols] = (dotx(far_ds, q, TN) * scale).astype(BF16)
+        back_v[:, cols] = dotx(far.astype(BF16), do, TN).astype(BF16)
+
+    backward = several(backward_head)
     load_w.wait()
     returned = []
     step_width = span_width // 2
@@ -539,7 +539,9 @@
             peer = peers[kind]
             total += dot(og_halves[peer // 2, peer % 2], w_in[kind, chunk, :, local])
         grad[:, cols] = total.astype(BF16)
-        lax.fori_loop(part * each // 2, (part + 1) * each // 2, backward, 0)
+        lax.fori_loop(
+            part * each // 2 // together, (part + 1) * each // 2 // together, backward, 0
+        )
         for kind in (PARTNER, DIAG, MATE):
             for out, into in ((back_k, came_k), (back_v, came_v)):
                 returned.append(

time: 85.1 us -> 83 us (0.975)
  Pallas kernels: 84.3 us -> 82.2 us
    pallas_call x1, Pallas kernels: 81.4 us -> 79.2 us  [fused(): pl.pallas_call(functools.partial(fused_kernel, slots, line), out_shape=[p...]
where the time goes in v6:
time: 83 us; the launch traced here: 82.8 us
  Pallas kernels  82.2 us (99%)
    pallas_call x1, Pallas kernels, fused(): pl.pallas_call(functools.partial(fused_kernel, slots, line), out_shape=[p...  79.2 us
    pallas_call x1, Pallas kernels, finish(): pl.pallas_call(finish_kernel, out_shape=[jax.ShapeDtypeStruct((rows, widt...  2.97 us

profile of v6, /device:TPU:1, one launch (start us, length us, event | category | flops | bytes accessed | tf_op | source)
XLA Modules:
  0.0 82.8 jit_solution(12682010244972916731)
XLA Ops:
  0.6 79.2 %shard_map.93 = (bf16[256,1536]{1,0:T(8,128)(2,1)S(1)}, bf16[256,1536]{1,0:T(8,128)(2,1)S(1)}, bf16[256,1536]{1,0:T(8,128)(2,1)S(1)}, f32[768,1536]{1,0:T(8,128)S(1)}) custom-call(s32[2,8]{1,0:T(2,128)} %lists_ref.1, bf16[256,1536]{1,0:T(8,128)(2,1)} %bitcast.7, bf16[256,1536]{1,0:T(8,128)(2,1)} %bitcast.8, bf16[256,1536]{1,0:T(8,128)(2,1)} %bitcast.9, ...), custom_call_target="tpu_custom_call" | custom-call | flops 7000000000 | bytes 16000000 | tf_op jit(solution)/shard_map/pallas_call | solution.py:646
  79.9 3.0 %shard_map.94 = (bf16[256,1536]{1,0:T(8,128)(2,1)}, bf16[256,1536]{1,0:T(8,128)(2,1)}, bf16[256,1536]{1,0:T(8,128)(2,1)}, f32[768,1536]{1,0:T(8,128)}) custom-call(bf16[256,1536]{1,0:T(8,128)(2,1)S(1)} %get-tuple-element.12.dq_ref, bf16[256,1536]{1,0:T(8,128)(2,1)S(1)} %get-tuple-element.13.dk_ref, bf16[256,1536]{1,0:T(8,128)(2,1)S(1)} %get-tuple-element.14.dv_ref, ...), custom_call_target="tpu_custom_call" | custom-call | bytes 7000000 | tf_op jit(solution)/shard_map/pallas_call | solution.py:617

commit v7 on v6

--- a/solution.py
+++ b/solution.py
@@ -487,12 +487,16 @@
     each = heads // chunks
     attn_partner = []
     attn_mate = []
-    for chunk in range(chunks):
-        lax.fori_loop(chunk * each // together, (chunk + 1) * each // together, forward, 0)
-        own = attn.at[SELF, :, chunk_cols(chunk)]
-        attn_mate.append(send(own, attn.at[MATE, :, chunk_cols(chunk)], to(MATE)))
-        attn_partner.append(send(own, attn.at[PARTNER, :, chunk_cols(chunk)], to(PARTNER)))
-        if chunk == 0:
+    part_width = span_width // 2
+    for part in range(2 * chunks):
+        lax.fori_loop(
+            part * each // 2 // together, (part + 1) * each // 2 // together, forward, 0
+        )
+        cols = pl.ds(part * part_width, part_width)
+        own = attn.at[SELF, :, cols]
+        attn_partner.append(send(own, attn.at[PARTNER, :, cols], to(PARTNER)))
+        attn_mate.append(send(own, attn.at[MATE, :, cols], to(MATE)))
+        if part == 1:
             hop_start(1, 2)
             hop_wait(0, 2)
     swapped = []
@@ -550,10 +554,10 @@
     came_k[0:far_rows, :] = back_k[0:far_rows, :]
     came_v[0:far_rows, :] = back_v[0:far_rows, :]
     attn_diag = []
-    for chunk in range(chunks):
-        attn_partner[chunk].wait_recv()
-        held = attn.at[PARTNER, :, chunk_cols(chunk)]
-        attn_diag.append(send(held, attn.at[DIAG, :, chunk_cols(chunk)], to(MATE)))
+    for part in range(2 * chunks):
+        attn_partner[part].wait_recv()
+        cols = pl.ds(part * part_width, part_width)
+        attn_diag.append(send(attn.at[PARTNER, :, cols], attn.at[DIAG, :, cols], to(MATE)))
     columns_in[MATE].wait_recv()
     for copy in swapped:
         copy.wait_recv()

time: 83 us -> 83.1 us (level)
  no operation moved by 1% of the time
where the time goes in v7:
time: 83.1 us; the launch traced here: 82.9 us
  Pallas kernels  82.1 us (99%)
    pallas_call x1, Pallas kernels, fused(): pl.pallas_call(functools.partial(fused_kernel, slots, line), out_shape=[p...  79.2 us
    pallas_call x1, Pallas kernels, finish(): pl.pallas_call(finish_kernel, out_shape=[jax.ShapeDtypeStruct((rows, widt...  2.97 us

profile of v7, /device:TPU:1, one launch (start us, length us, event | category | flops | bytes accessed | tf_op | source)
XLA Modules:
  0.0 82.9 jit_solution(15238502390832825248)
XLA Ops:
  0.6 79.2 %shard_map.93 = (bf16[256,1536]{1,0:T(8,128)(2,1)S(1)}, bf16[256,1536]{1,0:T(8,128)(2,1)S(1)}, bf16[256,1536]{1,0:T(8,128)(2,1)S(1)}, f32[768,1536]{1,0:T(8,128)S(1)}) custom-call(s32[2,8]{1,0:T(2,128)} %lists_ref.1, bf16[256,1536]{1,0:T(8,128)(2,1)} %bitcast.7, bf16[256,1536]{1,0:T(8,128)(2,1)} %bitcast.8, bf16[256,1536]{1,0:T(8,128)(2,1)} %bitcast.9, ...), custom_call_target="tpu_custom_call" | custom-call | flops 7000000000 | bytes 16000000 | tf_op jit(solution)/shard_map/pallas_call | solution.py:650
  79.8 3.0 %shard_map.94 = (bf16[256,1536]{1,0:T(8,128)(2,1)}, bf16[256,1536]{1,0:T(8,128)(2,1)}, bf16[256,1536]{1,0:T(8,128)(2,1)}, f32[768,1536]{1,0:T(8,128)}) custom-call(bf16[256,1536]{1,0:T(8,128)(2,1)S(1)} %get-tuple-element.12.dq_ref, bf16[256,1536]{1,0:T(8,128)(2,1)S(1)} %get-tuple-element.13.dk_ref, bf16[256,1536]{1,0:T(8,128)(2,1)S(1)} %get-tuple-element.14.dv_ref, ...), custom_call_target="tpu_custom_call" | custom-call | bytes 7000000 | tf_op jit(solution)/shard_map/pallas_call | solution.py:621
